TPU v7x, 512 devices: a whole 4x8x8 slice. The times are simulated.
512 devices in a mesh: seq: 32 (over z, x_hi, core), head: 16 (over y, x_lo).
Axes of the slice: x: 4 (x_hi: 2, x_lo: 2; x = x_hi * 2 + x_lo), y: 8, z: 8, core: 2. Of those that a mesh axis runs over, the one named last changes fastest.
Arguments:
- video_qkv: bfloat16 [65536, 3, 2048], P(('seq', 'head')), may hold values from -6 to 6
- audio_qkv: bfloat16 [8192, 3, 2048], P(('seq', 'head')), may hold values from -6 to 6
- pairs: int32 [32, 3], replicated, may hold values from 0 to 1, as said below
Outputs:
- video_out: bfloat16 [65536, 2048], P(('seq', 'head'))
- audio_out: bfloat16 [8192, 2048], P(('seq', 'head'))
Inputs may be any that keep to these rules, and one draw needn't show every extreme that they name: pairs[i, k] is 1 when video block i is paired with audio block i + k - 1; the middle column is always 1, and no pair names a block outside the 32 blocks.
All inputs are finite; a program needn't handle non-finite values.
Results may differ from a plain program's by a relative error of at most 0.009.
Values may be sent and summed in bfloat16 or wider, within the bound.
No kernel may reach another device: no remote copies, remote signals or barrier semaphores. Data moves between devices by JAX's collectives and lax.ppermute only.
A program may use at most 64 MiB of HBM per device.

v0:
```python
import math

import jax
import jax.numpy as jnp
from jax import lax
from jax.sharding import PartitionSpec as P

HD = 128


def padded(block, sides, width):
    for axis, dim in sides:
        count = lax.axis_size(axis)
        forward = [(i, i + 1) for i in range(count - 1)]
        backward = [(target, source) for source, target in forward]
        low = lax.ppermute(
            lax.slice_in_dim(block, block.shape[dim] - width, None, axis=dim), axis, forward
        )
        high = lax.ppermute(lax.slice_in_dim(block, 0, width, axis=dim), axis, backward)
        block = jnp.concatenate([low, block, high], axis=dim)
    return block


def partial_rows(queries, keys, values, valid):
    rows = queries.shape[0]
    block = math.gcd(rows, 512)
    scale = queries.shape[2] ** (-0.5)

    def one_block(block_queries):
        scores = (
            jnp.einsum("rhd,khd->hrk", block_queries, keys, preferred_element_type=jnp.float32)
            * scale
        )
        scores = jnp.where(valid[None, None, :], scores, -jnp.inf)
        largest = jnp.max(scores, axis=2)
        weights = jnp.exp(scores - largest[:, :, None])
        total = jnp.sum(weights, axis=2)
        summed = jnp.einsum(
            "hrk,khd->rhd", weights.astype(jnp.bfloat16), values, preferred_element_type=jnp.float32
        )
        return (summed, largest.T, total.T)

    blocked = queries.reshape(rows // block, block, queries.shape[1], queries.shape[2])
    summed, largest, total = lax.map(one_block, blocked)
    return (
        summed.reshape(rows, queries.shape[1], queries.shape[2]),
        largest.reshape(rows, queries.shape[1]),
        total.reshape(rows, queries.shape[1]),
    )


def finish(summed, total):
    return (summed / total[:, :, None]).astype(jnp.bfloat16).reshape(summed.shape[0], -1)


def on_device(video_qkv, audio_qkv, pairs):
    head_size = HD
    video_heads, audio_heads = (
        lax.all_to_all(video_qkv, "head", split_axis=2, concat_axis=0, tiled=True),
        lax.all_to_all(audio_qkv, "head", split_axis=2, concat_axis=0, tiled=True),
    )
    video_rows = video_heads.shape[0]
    audio_rows = audio_heads.shape[0]
    local_heads = video_heads.shape[2] // head_size
    video_split = video_heads.reshape(video_rows, 3, local_heads, head_size)
    audio_split = audio_heads.reshape(audio_rows, 3, local_heads, head_size)
    place = lax.axis_index("seq")
    padded_flags = jnp.pad(pairs, ((1, 1), (0, 0)))
    own_flags = lax.dynamic_index_in_dim(pairs, place, 0, keepdims=False) == 1
    moving = audio_heads[:, 1:]
    nearby = padded(moving, (("seq", 0),), audio_rows)
    width = moving.shape[1]
    nearby = nearby.reshape(3 * audio_rows, width, local_heads, head_size)
    video_keys = jnp.concatenate([video_split[:, 1], nearby[:, width - 2]], axis=0)
    video_values = jnp.concatenate([video_split[:, 2], nearby[:, width - 1]], axis=0)
    video_valid = jnp.concatenate(
        [jnp.ones((video_rows,), bool), jnp.repeat(own_flags, audio_rows)]
    )
    summed, largest, total = partial_rows(video_split[:, 0], video_keys, video_values, video_valid)
    video_result = finish(summed, total)
    distant = padded(video_heads[:, 1:], (("seq", 0),), video_rows)
    distant = distant.reshape(3 * video_rows, 2, local_heads, head_size)
    window = lax.dynamic_slice_in_dim(padded_flags, place, 3, 0)
    incoming = jnp.stack([window[0, 2], window[1, 1], window[2, 0]]) == 1
    audio_keys = jnp.concatenate([audio_split[:, 1], distant[:, 0]], axis=0)
    audio_values = jnp.concatenate([audio_split[:, 2], distant[:, 1]], axis=0)
    audio_valid = jnp.concatenate([jnp.ones((audio_rows,), bool), jnp.repeat(incoming, video_rows)])
    summed, largest, total = partial_rows(audio_split[:, 0], audio_keys, audio_values, audio_valid)
    audio_result = finish(summed, total)
    video_back, audio_back = (
        lax.all_to_all(video_result, "head", split_axis=0, concat_axis=1, tiled=True),
        lax.all_to_all(audio_result, "head", split_axis=0, concat_axis=1, tiled=True),
    )
    return (video_back, audio_back)


def solution(mesh):
    return jax.shard_map(
        on_device,
        mesh=mesh,
        in_specs=(P(("seq", "head"), None, None), P(("seq", "head"), None, None), P()),
        out_specs=(P(("seq", "head"), None), P(("seq", "head"), None)),
        check_vma=False,
    )
```

profile of v0, /device:TPU:448, one launch (start us, length us, event | category | flops | bytes accessed | tf_op | source)
XLA Modules:
  0.0 143.4 jit_solution(6066339412394647473)
XLA Ops:
  0.6 2.6 %copy.39 = bf16[16,3,2048]{0,1,2:T(4,128)(2,1)S(1)} copy(bf16[16,3,2048]{2,0,1:T(8,128)(2,1)} %param.6) | data formatting | bytes 393216 | tf_op args[1]
  3.2 2.7 %reshape.140 = bf16[16,2,3072]{2,1,0:T(2,128)(2,1)} reshape(bf16[2048,3,16]{2,1,0:T(4,128)(2,1)S(1)} %bitcast.124) | data formatting | bytes 393216
  5.9 8.1 %all-to-all-start.1 = ((bf16[16,2,3072]{2,1,0:T(2,128)(2,1)}), bf16[16,2,3072]{2,1,0:T(2,128)(2,1)S(1)}, u32[]{:S(2)}, u32[]{:S(2)}) async-start(bf16[16,2,3072]{2,1,0:T(2,128)(2,1)} %reshape.140), calls=%async_computation.1 | async-start | bytes 393216 | tf_op jit(solution)/shard_map/all_to_all | solution.py:60
  14.1 4.2 %copy.37 = bf16[128,3,2048]{0,1,2:T(4,128)(2,1)} copy(bf16[128,3,2048]{2,0,1:T(8,128)(2,1)} %param.5) | data formatting | bytes 3145728 | tf_op args[0]
  18.3 6.7 %all-to-all-done.1 = bf16[16,2,3072]{2,1,0:T(2,128)(2,1)S(1)} async-done(((bf16[16,2,3072]{2,1,0:T(2,128)(2,1)}), bf16[16,2,3072]{2,1,0:T(2,128)(2,1)S(1)}, u32[]{:S(2)}, u32[]{:S(2)}) %all-to-all-start.1) | async-done | bytes 196640 | tf_op jit(solution)/shard_map/all_to_all | solution.py:60
  24.9 3.7 %all-to-all-start = ((bf16[128,3,2048]{0,1,2:T(4,128)(2,1)}), bf16[128,3,2048]{0,1,2:T(4,128)(2,1)S(1)}, u32[]{:S(2)}, u32[]{:S(2)}) async-start(bf16[128,3,2048]{0,1,2:T(4,128)(2,1)} %copy.37), calls=%async_computation | async-start | bytes 4194304 | tf_op jit(solution)/shard_map/all_to_all | solution.py:59
  29.4 2.0 %add_compare_fusion = pred[3]{0:T(512)(128)(4,1)S(1)} fusion(s32[1]{0:T(128)} %bitcast.35, s32[1]{0:T(128)} %bitcast.34, s32[1]{0:T(128)} %bitcast.33), kind=kLoop, calls=%fused_computation.53 | loop fusion | flops 9 | bytes 15 | tf_op jit(solution)/shard_map/eq | solution.py:84
  32.4 3.0 %reshape.141 = bf16[2048,3,16]{2,1,0:T(4,128)(2,1)} reshape(bf16[16,2,3072]{2,1,0:T(2,128)(2,1)S(1)} %all-to-all-done.1) | data formatting | bytes 393216
  35.5 2.8 %copy.40 = bf16[16,3,16,128]{3,0,2,1:T(8,128)(2,1)S(1)} copy(bf16[16,3,16,128]{0,1,3,2:T(4,128)(2,1)} %bitcast.123) | data formatting | bytes 393216 | tf_op jit(solution)/shard_map/all_to_all | solution.py:60
  38.2 1.9 %collective-permute-start = (bf16[256,2,128]{2,0,1:T(8,128)(2,1)S(1)}, bf16[256,2,128]{2,0,1:T(8,128)(2,1)S(1)}, u32[]{:S(2)}, u32[]{:S(2)}) collective-permute-start(bf16[256,2,128]{2,0,1:T(8,128)(2,1)S(1)} %slice.62), channel_id=1, source_target_pairs={{0,16},{16,32},{32,48},{48,64},{64,80},{80,96},{96,112},{112,128},... | collective-permute-start | bytes 393224 | tf_op jit(solution)/shard_map/ppermute | solution.py:16
  40.2 6.0 %collective-permute-start.1 = (bf16[256,2,128]{2,0,1:T(8,128)(2,1)S(1)}, bf16[256,2,128]{2,0,1:T(8,128)(2,1)S(1)}, u32[]{:S(2)}, u32[]{:S(2)}) collective-permute-start(bf16[256,2,128]{2,0,1:T(8,128)(2,1)S(1)} %slice.62), channel_id=1, source_target_pairs={{16,0},{32,16},{48,32},{64,48},{80,64},{96,80},{112,96},{128,112},... | collective-permute-start | bytes 393224 | tf_op jit(solution)/shard_map/ppermute | solution.py:19
  47.2 1.6 %collective-permute-done.1 = bf16[256,2,128]{2,0,1:T(8,128)(2,1)S(1)} collective-permute-done((bf16[256,2,128]{2,0,1:T(8,128)(2,1)S(1)}, bf16[256,2,128]{2,0,1:T(8,128)(2,1)S(1)}, u32[]{:S(2)}, u32[]{:S(2)}) %collective-permute-start.1) | collective-permute-done | bytes 131104 | tf_op jit(solution)/shard_map/ppermute | solution.py:19
  49.5 28.1 %all-to-all-done = bf16[128,3,2048]{0,1,2:T(4,128)(2,1)S(1)} async-done(((bf16[128,3,2048]{0,1,2:T(4,128)(2,1)}), bf16[128,3,2048]{0,1,2:T(4,128)(2,1)S(1)}, u32[]{:S(2)}, u32[]{:S(2)}) %all-to-all-start) | async-done | bytes 1572896 | tf_op jit(solution)/shard_map/all_to_all | solution.py:59
  77.6 1.3 copy-done
  78.9 3.0 %copy.38 = bf16[128,3,16,128]{3,0,2,1:T(8,128)(2,1)S(1)} copy(bf16[128,3,16,128]{0,1,3,2:T(4,128)(2,1)} %bitcast.122) | data formatting | bytes 3145728 | tf_op jit(solution)/shard_map/all_to_all | solution.py:59
  82.0 1.9 %collective-permute-start.2 = (bf16[2048,2,128]{2,0,1:T(8,128)(2,1)S(1)}, bf16[2048,2,128]{2,0,1:T(8,128)(2,1)}, u32[]{:S(2)}, u32[]{:S(2)}) collective-permute-start(bf16[2048,2,128]{2,0,1:T(8,128)(2,1)S(1)} %slice.67), channel_id=1, source_target_pairs={{0,16},{16,32},{32,48},{48,64},{64,80},{80,96},{96,112},{112,128},... | collective-permute-start | bytes 3145736 | tf_op jit(solution)/shard_map/ppermute | solution.py:16
  84.0 6.0 %collective-permute-start.3 = (bf16[2048,2,128]{2,0,1:T(8,128)(2,1)S(1)}, bf16[2048,2,128]{2,0,1:T(8,128)(2,1)}, u32[]{:S(2)}, u32[]{:S(2)}) collective-permute-start(bf16[2048,2,128]{2,0,1:T(8,128)(2,1)S(1)} %slice.67), channel_id=1, source_target_pairs={{16,0},{32,16},{48,32},{64,48},{80,64},{96,80},{112,96},{128,112},... | collective-permute-start | bytes 3145736 | tf_op jit(solution)/shard_map/ppermute | solution.py:19
  90.2 17.2 %while.2 = (s32[]{:T(128)}, f32[4,512,1,128]{3,1,2,0:T(8,128)}, f32[4,512,1]{1,2,0:T(1,128)S(1)}, pred[2816]{0:T(1024)(128)(4,1)S(1)}, bf16[4,512,1,128]{3,1,2,0...) while((s32[]{:T(128)}, f32[4,512,1,128]{3,1,2,0:T(8,128)}, ...), condition=%wide.region_3.4_spmd, body=%wide.region_0.3_spmd.sunk | while | flops 754056192 | bytes 19158108 | solution.py:44
  91.3 1.3 fusion.57
  92.6 1.9 %fusion.56 = f32[4,512,1,128]{3,1,2,0:T(8,128)} fusion(f32[4,512,1,128]{3,1,2,0:T(8,128)} %get-tuple-element.188, s32[]{:T(128)} %get-tuple-element.187, f32[512,2816]{1,0:T(8,128)S(1)} %get-tuple-element.177, f32[512]{0:T(512)S(1)} %get-tuple-element.178, pred[2816]{0:T(1024)(128)(4,1)S(1)} %get-tuple-element.198, ...), kind=kOutput, calls=%fused_computation.8.clone.1 | convolution fusion | flops 374865920 | bytes 6755584 | tf_op jit(solution)/shard_map/while/body/eval_jaxpr/hrk,khd->rhd/dot_general | solution.py:38
  95.6 1.3 fusion.57
  96.9 2.0 %fusion.56 = f32[4,512,1,128]{3,1,2,0:T(8,128)} fusion(f32[4,512,1,128]{3,1,2,0:T(8,128)} %get-tuple-element.188, s32[]{:T(128)} %get-tuple-element.187, f32[512,2816]{1,0:T(8,128)S(1)} %get-tuple-element.177, f32[512]{0:T(512)S(1)} %get-tuple-element.178, pred[2816]{0:T(1024)(128)(4,1)S(1)} %get-tuple-element.198, ...), kind=kOutput, calls=%fused_computation.8.clone.1 | convolution fusion | flops 374865920 | bytes 6755584 | tf_op jit(solution)/shard_map/while/body/eval_jaxpr/hrk,khd->rhd/dot_general | solution.py:38
  99.9 1.3 fusion.57
  101.2 2.0 %fusion.56 = f32[4,512,1,128]{3,1,2,0:T(8,128)} fusion(f32[4,512,1,128]{3,1,2,0:T(8,128)} %get-tuple-element.188, s32[]{:T(128)} %get-tuple-element.187, f32[512,2816]{1,0:T(8,128)S(1)} %get-tuple-element.177, f32[512]{0:T(512)S(1)} %get-tuple-element.178, pred[2816]{0:T(1024)(128)(4,1)S(1)} %get-tuple-element.198, ...), kind=kOutput, calls=%fused_computation.8.clone.1 | convolution fusion | flops 374865920 | bytes 6755584 | tf_op jit(solution)/shard_map/while/body/eval_jaxpr/hrk,khd->rhd/dot_general | solution.py:38
  105.5 1.9 %fusion.56 = f32[4,512,1,128]{3,1,2,0:T(8,128)} fusion(f32[4,512,1,128]{3,1,2,0:T(8,128)} %get-tuple-element.188, s32[]{:T(128)} %get-tuple-element.187, f32[512,2816]{1,0:T(8,128)S(1)} %get-tuple-element.177, f32[512]{0:T(512)S(1)} %get-tuple-element.178, pred[2816]{0:T(1024)(128)(4,1)S(1)} %get-tuple-element.198, ...), kind=kOutput, calls=%fused_computation.8.clone.1 | convolution fusion | flops 374865920 | bytes 6755584 | tf_op jit(solution)/shard_map/while/body/eval_jaxpr/hrk,khd->rhd/dot_general | solution.py:38
  107.4 2.4 %divide_convert_fusion = bf16[16,128,128]{2,1,0:T(8,128)(2,1)} fusion(f32[16,128,128]{2,1,0:T(8,128)} %bitcast.22, f32[16,128]{1,0:T(8,128)S(1)} %bitcast.131), kind=kLoop, calls=%fused_computation.38 | loop fusion | flops 524288 | bytes 1581056 | tf_op jit(solution)/shard_map/convert_element_type | solution.py:53
  109.8 3.6 %all-to-all-start.2 = ((bf16[16,128,128]{2,1,0:T(8,128)(2,1)}), bf16[16,128,128]{2,1,0:T(8,128)(2,1)S(1)}, u32[]{:S(2)}, u32[]{:S(2)}) async-start(bf16[16,128,128]{2,1,0:T(8,128)(2,1)} %divide_convert_fusion), calls=%async_computation.2 | async-start | bytes 1048576 | tf_op jit(solution)/shard_map/all_to_all | solution.py:91
  113.4 1.7 %maximum_bitcast_fusion = bf16[6144,2,1,128]{3,0,1,2:T(8,128)(2,1)S(1)} fusion(bf16[2048,2,128]{2,0,1:T(8,128)(2,1)} %collective-permute-done.3, bf16[2048,2,128]{2,0,1:T(8,128)(2,1)S(1)} %slice.67, bf16[2048,2,128]{2,0,1:T(8,128)(2,1)} %collective-permute-done.2), kind=kLoop, calls=%fused_computation.25 | loop fusion | flops 9437184 | bytes 6291456 | tf_op jit(solution)/shard_map/reshape | solution.py:82
  115.9 1.4 fusion.46
  120.2 9.9 %all-to-all-done.2 = bf16[16,128,128]{2,1,0:T(8,128)(2,1)S(1)} async-done(((bf16[16,128,128]{2,1,0:T(8,128)(2,1)}), bf16[16,128,128]{2,1,0:T(8,128)(2,1)S(1)}, u32[]{:S(2)}, u32[]{:S(2)}) %all-to-all-start.2) | async-done | bytes 524320 | tf_op jit(solution)/shard_map/all_to_all | solution.py:91
  130.2 3.5 %all-to-all-start.3 = ((bf16[16,16,128]{2,1,0:T(8,128)(2,1)}), bf16[16,16,128]{2,1,0:T(8,128)(2,1)S(1)}, u32[]{:S(2)}, u32[]{:S(2)}) async-start(bf16[16,16,128]{2,1,0:T(8,128)(2,1)} %bitcast.44), calls=%async_computation.3 | async-start | bytes 131072 | tf_op jit(solution)/shard_map/all_to_all | solution.py:92
  135.0 7.8 %all-to-all-done.3 = bf16[16,16,128]{2,1,0:T(8,128)(2,1)S(1)} async-done(((bf16[16,16,128]{2,1,0:T(8,128)(2,1)}), bf16[16,16,128]{2,1,0:T(8,128)(2,1)S(1)}, u32[]{:S(2)}, u32[]{:S(2)}) %all-to-all-start.3) | async-done | bytes 65568 | tf_op jit(solution)/shard_map/all_to_all | solution.py:92
  (48 shorter events, 14.9 us)
Async XLA Ops:
  5.9 19.0 %all-to-all-start.1 = ((bf16[16,2,3072]{2,1,0:T(2,128)(2,1)}), bf16[16,2,3072]{2,1,0:T(2,128)(2,1)S(1)}, u32[]{:S(2)}, u32[]{:S(2)}) async-start(bf16[16,2,3072]{2,1,0:T(2,128)(2,1)} %reshape.140), calls=%async_computation.1 | async-start | bytes 393216 | tf_op jit(solution)/shard_map/all_to_all | solution.py:60
  14.1 14.6 %copy-start.4 = (s32[32,3]{0,1:T(4,128)S(1)}, s32[32,3]{0,1:T(4,128)}, u32[]{:S(2)}) copy-start(s32[32,3]{0,1:T(4,128)} %param.7) | copy-start | bytes 1156
  24.9 52.6 %all-to-all-start = ((bf16[128,3,2048]{0,1,2:T(4,128)(2,1)}), bf16[128,3,2048]{0,1,2:T(4,128)(2,1)S(1)}, u32[]{:S(2)}, u32[]{:S(2)}) async-start(bf16[128,3,2048]{0,1,2:T(4,128)(2,1)} %copy.37), calls=%async_computation | async-start | bytes 4194304 | tf_op jit(solution)/shard_map/all_to_all | solution.py:59
  38.2 8.9 %collective-permute-start = (bf16[256,2,128]{2,0,1:T(8,128)(2,1)S(1)}, bf16[256,2,128]{2,0,1:T(8,128)(2,1)S(1)}, u32[]{:S(2)}, u32[]{:S(2)}) collective-permute-start(bf16[256,2,128]{2,0,1:T(8,128)(2,1)S(1)} %slice.62), channel_id=1, source_target_pairs={{0,16},{16,32},{32,48},{48,64},{64,80},{80,96},{96,112},{112,128},... | collective-permute-start | bytes 393224 | tf_op jit(solution)/shard_map/ppermute | solution.py:16
  40.2 8.6 %collective-permute-start.1 = (bf16[256,2,128]{2,0,1:T(8,128)(2,1)S(1)}, bf16[256,2,128]{2,0,1:T(8,128)(2,1)S(1)}, u32[]{:S(2)}, u32[]{:S(2)}) collective-permute-start(bf16[256,2,128]{2,0,1:T(8,128)(2,1)S(1)} %slice.62), channel_id=1, source_target_pairs={{16,0},{32,16},{48,32},{64,48},{80,64},{96,80},{112,96},{128,112},... | collective-permute-start | bytes 393224 | tf_op jit(solution)/shard_map/ppermute | solution.py:19
  77.6 1.3 copy-start
  81.9 8.2 %copy-start.1 = (bf16[768,1,128]{2,0,1:T(8,128)(2,1)S(1)}, bf16[768,1,128]{2,0,1:T(8,128)(2,1)}, u32[]{:S(2)}) copy-start(bf16[768,1,128]{2,0,1:T(8,128)(2,1)} %get-tuple-element.122) | copy-start | bytes 589828
  82.0 31.4 %collective-permute-start.2 = (bf16[2048,2,128]{2,0,1:T(8,128)(2,1)S(1)}, bf16[2048,2,128]{2,0,1:T(8,128)(2,1)}, u32[]{:S(2)}, u32[]{:S(2)}) collective-permute-start(bf16[2048,2,128]{2,0,1:T(8,128)(2,1)S(1)} %slice.67), channel_id=1, source_target_pairs={{0,16},{16,32},{32,48},{48,64},{64,80},{80,96},{96,112},{112,128},... | collective-permute-start | bytes 3145736 | tf_op jit(solution)/shard_map/ppermute | solution.py:16
  84.0 29.4 %collective-permute-start.3 = (bf16[2048,2,128]{2,0,1:T(8,128)(2,1)S(1)}, bf16[2048,2,128]{2,0,1:T(8,128)(2,1)}, u32[]{:S(2)}, u32[]{:S(2)}) collective-permute-start(bf16[2048,2,128]{2,0,1:T(8,128)(2,1)S(1)} %slice.67), channel_id=1, source_target_pairs={{16,0},{32,16},{48,32},{64,48},{80,64},{96,80},{112,96},{128,112},... | collective-permute-start | bytes 3145736 | tf_op jit(solution)/shard_map/ppermute | solution.py:19
  109.8 20.4 %all-to-all-start.2 = ((bf16[16,128,128]{2,1,0:T(8,128)(2,1)}), bf16[16,128,128]{2,1,0:T(8,128)(2,1)S(1)}, u32[]{:S(2)}, u32[]{:S(2)}) async-start(bf16[16,128,128]{2,1,0:T(8,128)(2,1)} %divide_convert_fusion), calls=%async_computation.2 | async-start | bytes 1048576 | tf_op jit(solution)/shard_map/all_to_all | solution.py:91
  115.1 0.8 copy-start.3
  115.1 0.8 copy-start.5
  117.3 1.0 copy-start.2
  130.2 12.6 %all-to-all-start.3 = ((bf16[16,16,128]{2,1,0:T(8,128)(2,1)}), bf16[16,16,128]{2,1,0:T(8,128)(2,1)S(1)}, u32[]{:S(2)}, u32[]{:S(2)}) async-start(bf16[16,16,128]{2,1,0:T(8,128)(2,1)} %bitcast.44), calls=%async_computation.3 | async-start | bytes 131072 | tf_op jit(solution)/shard_map/all_to_all | solution.py:92
where the time goes:
time: 145 us; the launch traced here: 143 us
  waiting for transfers between devices  54.4 us (38%)
  starting transfers between devices  34.9 us (24%)
  local copies, waits for them, and re-layouts  26.2 us (18%)
  matrix products  14.6 us (10%)
  other arithmetic  12.5 us (9%)
    all_to_all x1, waiting for transfers between devices, on_device(): lax.all_to_all(video_qkv, 'head', split_axis=2, concat_axis=0, tiled=True)  28.1 us
    unnamed x17, local copies, waits for them, and re-layouts  15.5 us
    ppermute x2, starting transfers between devices, padded(): lax.ppermute(lax.slice_in_dim(block, 0, width, axis=dim), axis, backward)  12.1 us
    all_to_all x1, waiting for transfers between devices, on_device(): lax.all_to_all(video_result, 'head', split_axis=0, concat_axis=1, tiled=T...  9.94 us
    dot_general x5, matrix products, one_block(): jnp.einsum('hrk,khd->rhd', weights.astype(jnp.bfloat16), values, preferre...  9.09 us
    all_to_all x1, starting transfers between devices, on_device(): lax.all_to_all(audio_qkv, 'head', split_axis=2, concat_axis=0, tiled=True)  8.13 us
    all_to_all x1, waiting for transfers between devices, on_device(): lax.all_to_all(audio_result, 'head', split_axis=0, concat_axis=1, tiled=T...  7.76 us
    all_to_all x1, waiting for transfers between devices, on_device(): lax.all_to_all(audio_qkv, 'head', split_axis=2, concat_axis=0, tiled=True)  6.69 us
  transfers between devices with their start and end apart: 8, of which 6 were waited for; matrix products, arithmetic and copies ran while one was open for 29% of the time, Pallas kernels for 0%

commit v1 on v0

v1 whole, which is shorter than its diff:
```python
import math

import jax
import jax.numpy as jnp
from jax import lax
from jax.experimental import pallas as pl
from jax.experimental.pallas import tpu as pltpu
from jax.sharding import PartitionSpec as P

HD = 128
PEERS = 16
BLOCKS = 32
VT, AT = 128, 16
VB, AB = PEERS * VT, PEERS * AT
KEYS = VB + 3 * AB
STEP = 256
SCALE = math.log2(math.e) / math.sqrt(HD)
VMEM_LIMIT = 48 << 20
BF16, F32 = jnp.bfloat16, jnp.float32
ON_ROWS = (((1,), (1,)), ((), ()))


def rows(ref, part, low, high):
    return ref[:, part, low:high].reshape(PEERS * (high - low), HD)


def stage(place, sources, keys, values):
    for low, (ref, first, last) in zip(place, sources):
        part = ref[:, 1, first:last].reshape(-1, HD)
        keys[low : low + part.shape[0]] = part
        values[low : low + part.shape[0], 0:HD] = ref[:, 2, first:last].reshape(-1, HD)
    values[:, HD : 2 * HD] = jnp.ones((values.shape[0], HD), BF16)


def score(queries, keys, buffer, columns, bias):
    largest = None
    for place, j in enumerate(columns):
        part = lax.dot_general(
            queries, keys[j * STEP : (j + 1) * STEP], ON_ROWS, preferred_element_type=F32
        )
        if j in bias:
            part = part + bias[j]
        buffer[:, place * STEP : (place + 1) * STEP] = part
        for t in range(0, STEP, HD):
            lanes = part[:, t : t + HD]
            largest = lanes if largest is None else jnp.maximum(largest, lanes)
    return jnp.max(largest, axis=1, keepdims=True) * SCALE


def weigh(buffer, columns, largest, values):
    low, high = columns[0] * STEP, (columns[-1] + 1) * STEP
    scores = buffer[:, 0 : high - low]
    weights = jnp.exp2(scores * SCALE - largest).astype(BF16)
    summed = jnp.dot(weights, values[low:high], preferred_element_type=F32)
    return summed[:, :HD], summed[:, HD:]


def pipelined(jobs, buffers, keys, values):
    pending = None
    for index, (load, columns, bias, finish) in enumerate(jobs):
        buffer = buffers.at[index % 2]
        largest = score(load(), keys, buffer, columns, bias)
        if pending is not None:
            pending()

        def pending(buffer=buffer, columns=columns, largest=largest, finish=finish):
            summed, total = weigh(buffer, columns, largest, values)
            finish(summed, total, largest)

    pending()


def pack_kernel(video, audio, out):
    for h in range(PEERS):
        out[h, :, 0:VT] = video[:, :, h * HD : (h + 1) * HD]
        out[h, :, VT:] = audio[:, :, h * HD : (h + 1) * HD]


def unpack_kernel(heads, video, audio):
    for h in range(PEERS):
        video[:, h * HD : (h + 1) * HD] = heads[h, 0:VT]
        audio[:, h * HD : (h + 1) * HD] = heads[h, VT:]


def lend_kernel(own, left, right, to_left, to_right, keys, values, buffers):
    stage((0,), ((own, 0, VT),), keys, values)
    lane = lax.broadcasted_iota(jnp.int32, (AB, HD), 1)

    def job(source, out):
        def finish(summed, total, largest):
            out[0] = (summed / total).astype(BF16)
            level = largest + jnp.log2(total)
            high = level.astype(BF16)
            rest = level - high.astype(F32)
            middle = rest.astype(BF16)
            low = (rest - middle.astype(F32)).astype(BF16)
            out[1] = jnp.where(
                lane < 32, high.astype(F32), jnp.where(lane < 64, middle.astype(F32), low.astype(F32))
            ).astype(BF16)

        return (lambda: rows(source, 0, 0, AT), tuple(range(VB // STEP)), {}, finish)

    pipelined([job(left, to_left), job(right, to_right)], buffers, keys, values)


def main_kernel(pairs, own, left, right, out, audio, level, keys, values, buffers):
    place = lax.axis_index("seq")
    stage(
        (0, VB, VB + AB, VB + 2 * AB),
        ((own, 0, VT), (own, VT, VT + AT), (left, 0, AT), (right, 0, AT)),
        keys,
        values,
    )
    first = VB // STEP + 1
    bias = {
        first: jnp.where(pairs[place, 0] == 1, 0.0, -jnp.inf).astype(F32),
        first + 1: jnp.where(pairs[place, 2] == 1, 0.0, -jnp.inf).astype(F32),
    }
    count = STEP // VT

    def video_job(i):
        def finish(summed, total, largest):
            result = (summed / total).astype(BF16)
            out[i * count : (i + 1) * count, 0:VT] = result.reshape(count, VT, HD)

        return (
            lambda: own[i * count : (i + 1) * count, 0, 0:VT].reshape(STEP, HD),
            tuple(range(KEYS // STEP)),
            bias,
            finish,
        )

    def audio_finish(summed, total, largest):
        audio[...] = summed / total
        level[...] = largest + jnp.log2(total)

    audio_job = (
        lambda: rows(own, 0, VT, VT + AT),
        tuple(range(VB // STEP + 1)),
        {},
        audio_finish,
    )
    pipelined(
        [audio_job] + [video_job(i) for i in range(VB // STEP)], buffers, keys, values
    )


def merge_kernel(pairs, audio, level, from_left, from_right, unused, out):
    place = lax.axis_index("seq")
    left = (place > 0) & (pairs[jnp.maximum(place - 1, 0), 2] == 1)
    right = (place < BLOCKS - 1) & (pairs[jnp.minimum(place + 1, BLOCKS - 1), 0] == 1)

    def level_of(ref, valid):
        split = ref[1].astype(F32)
        value = split[:, 0:1] + split[:, 32:33] + split[:, 64:65]
        return value + jnp.where(valid, 0.0, -jnp.inf).astype(F32)

    levels = [level[:, 0:1], level_of(from_left, left), level_of(from_right, right)]
    largest = jnp.maximum(jnp.maximum(levels[0], levels[1]), levels[2])
    shares = [jnp.exp2(l - largest) for l in levels]
    summed = (
        shares[0] * audio[...]
        + shares[1] * from_left[0].astype(F32)
        + shares[2] * from_right[0].astype(F32)
    )
    result = summed / (shares[0] + shares[1] + shares[2])
    out[...] = result.astype(BF16).reshape(PEERS, AT, HD)


IN_VMEM = pl.BlockSpec(memory_space=pltpu.VMEM)
IN_SMEM = pl.BlockSpec(memory_space=pltpu.SMEM)


def cost(rows_, keys_, moved):
    return pl.CostEstimate(
        flops=4 * rows_ * keys_ * HD, bytes_accessed=moved, transcendentals=rows_ * keys_
    )


def scratch(keys_):
    return [
        pltpu.VMEM((keys_, HD), BF16),
        pltpu.VMEM((keys_, 2 * HD), BF16),
        pltpu.VMEM((2, STEP, keys_), F32),
    ]


def on_device(video_qkv, audio_qkv, pairs):
    params = pltpu.CompilerParams(vmem_limit_bytes=VMEM_LIMIT)
    tokens = pl.pallas_call(
        pack_kernel,
        out_shape=jax.ShapeDtypeStruct((PEERS, 3, VT + AT, HD), BF16),
        in_specs=[IN_VMEM] * 2,
        out_specs=IN_VMEM,
        compiler_params=params,
        name="pack",
    )(video_qkv.transpose(1, 0, 2), audio_qkv.transpose(1, 0, 2))
    own = lax.all_to_all(tokens, "head", split_axis=0, concat_axis=0, tiled=True)
    forward = [(i, i + 1) for i in range(BLOCKS - 1)]
    backward = [(i + 1, i) for i in range(BLOCKS - 1)]
    own_audio = own[:, :, VT:]
    left = lax.ppermute(own_audio, "seq", forward)
    right = lax.ppermute(own_audio, "seq", backward)
    part = jax.ShapeDtypeStruct((2, AB, HD), BF16)
    to_left, to_right = pl.pallas_call(
        lend_kernel,
        out_shape=(part, part),
        in_specs=[IN_VMEM] * 3,
        out_specs=(IN_VMEM, IN_VMEM),
        scratch_shapes=scratch(VB),
        compiler_params=params,
        cost_estimate=cost(2 * AB, VB, 2 << 20),
        name="lend",
    )(own, left, right)
    from_left = lax.ppermute(to_right, "seq", forward)
    from_right = lax.ppermute(to_left, "seq", backward)
    packed = jax.ShapeDtypeStruct((PEERS, VT + AT, HD), BF16)
    single = jax.ShapeDtypeStruct((AB, HD), F32)
    out, audio, level = pl.pallas_call(
        main_kernel,
        out_shape=(packed, single, single),
        in_specs=[IN_SMEM] + [IN_VMEM] * 3,
        out_specs=(IN_VMEM,) * 3,
        scratch_shapes=scratch(KEYS),
        compiler_params=params,
        cost_estimate=cost(VB + AB, KEYS, 3 << 20),
        name="attend",
    )(pairs, own, left, right)
    rows_of_audio = pl.BlockSpec((PEERS, AT, HD), lambda i: (0, VT // AT, 0))
    out = pl.pallas_call(
        merge_kernel,
        out_shape=packed,
        grid=(1,),
        in_specs=[IN_SMEM] + [IN_VMEM] * 4 + [pl.BlockSpec(memory_space=pl.ANY)],
        out_specs=rows_of_audio,
        input_output_aliases={5: 0},
        compiler_params=params,
        name="merge",
    )(pairs, audio, level, from_left, from_right, out)
    back = lax.all_to_all(out, "head", split_axis=0, concat_axis=0, tiled=True)
    return pl.pallas_call(
        unpack_kernel,
        out_shape=(
            jax.ShapeDtypeStruct((VT, PEERS * HD), BF16),
            jax.ShapeDtypeStruct((AT, PEERS * HD), BF16),
        ),
        in_specs=[IN_VMEM],
        out_specs=(IN_VMEM, IN_VMEM),
        compiler_params=params,
        name="unpack",
    )(back)


def solution(mesh):
    return jax.shard_map(
        on_device,
        mesh=mesh,
        in_specs=(P(("seq", "head"), None, None), P(("seq", "head"), None, None), P()),
        out_specs=(P(("seq", "head"), None), P(("seq", "head"), None)),
        check_vma=False,
    )
```

time: 145 us -> 112 us (0.77)
  the two profiles are of different devices: /device:TPU:448 before, /device:TPU:196 now
where the time goes in v1:
time: 112 us
  blocking collectives  75.4 us (67%)
  starting transfers between devices  17.1 us (15%)
  Pallas kernels  13 us (12%)
  waiting for transfers between devices  3.07 us (3%)
  local copies, waits for them, and re-layouts  2.44 us (2%)
    all_to_all x1, blocking collectives, on_device(): lax.all_to_all(tokens, 'head', split_axis=0, concat_axis=0, tiled=True)  52.2 us
    all_to_all x1, blocking collectives, on_device(): back = lax.all_to_all(out, 'head', split_axis=0, concat_axis=0, tiled=True)  23.2 us
    pallas_call x1, Pallas kernels, on_device(): pl.pallas_call(main_kernel, out_shape=(packed, single, single), in_specs=...  8.85 us
    ppermute x1, starting transfers between devices, on_device(): from_left = lax.ppermute(to_right, 'seq', forward)  8.12 us
    ppermute x1, starting transfers between devices, on_device(): right = lax.ppermute(own_audio, 'seq', backward)  5.15 us
    unnamed x7, local copies, waits for them, and re-layouts  2.42 us
  transfers between devices with their start and end apart: 4, of which 2 were waited for; matrix products, arithmetic and copies ran while one was open for 0% of the time, Pallas kernels for 8%

profile of v1, /device:TPU:196, one launch (start us, length us, event | category | flops | bytes accessed | tf_op | source)
XLA Modules:
  0.0 111.7 jit_solution(6439656617579247113)
XLA Ops:
  0.6 0.0 copy-start
  0.6 1.4 %copy-done = bf16[128,3,2048]{2,0,1:T(8,128)(2,1)S(1)} copy-done((bf16[128,3,2048]{2,0,1:T(8,128)(2,1)S(1)}, bf16[128,3,2048]{2,0,1:T(8,128)(2,1)}, u32[]{:S(2)}) %copy-start) | copy-done | bytes 1572888
  2.0 0.0 copy-start.1
  2.0 0.9 copy-done.1
  3.0 0.3 pack.1
  3.3 0.0 copy-start.2
  3.3 52.2 %all_to_all.10.own = bf16[16,3,144,128]{3,2,1,0:T(8,128)(2,1)S(1)} all-to-all(bf16[16,3,144,128]{3,2,1,0:T(8,128)(2,1)S(1)} %pack.1), channel_id=1, replica_groups=mesh['seq'=32,'head'=16] {'head'}, dimensions={0} | all-to-all | bytes 3538944 | tf_op jit(solution)/shard_map/all_to_all | solution.py:198
  55.5 1.9 %collective-permute-start = (bf16[16,3,16,128]{3,2,1,0:T(8,128)(2,1)S(1)}, bf16[16,3,16,128]{3,2,1,0:T(8,128)(2,1)S(1)}, u32[]{:S(2)}, u32[]{:S(2)}) collective-permute-start(bf16[16,3,16,128]{3,2,1,0:T(8,128)(2,1)S(1)} %slice.4), channel_id=1, source_target_pairs={{0,16},{16,32},{32,48},{48,64},{64,80},{80,96},{96,112},{112,128},... | collective-permute-start | bytes 589832 | tf_op jit(solution)/shard_map/ppermute | solution.py:202
  57.5 5.1 %collective-permute-start.1 = (bf16[16,3,16,128]{3,2,1,0:T(8,128)(2,1)S(1)}, bf16[16,3,16,128]{3,2,1,0:T(8,128)(2,1)S(1)}, u32[]{:S(2)}, u32[]{:S(2)}) collective-permute-start(bf16[16,3,16,128]{3,2,1,0:T(8,128)(2,1)S(1)} %slice.4), channel_id=1, source_target_pairs={{16,0},{32,16},{48,32},{64,48},{80,64},{96,80},{112,96},{128,112},... | collective-permute-start | bytes 589832 | tf_op jit(solution)/shard_map/ppermute | solution.py:203
  62.6 0.0 copy-done.2
  62.6 0.1 copy.7.pairs
  62.7 1.3 %collective-permute-done.left = bf16[16,3,16,128]{3,2,1,0:T(8,128)(2,1)S(1)} collective-permute-done((bf16[16,3,16,128]{3,2,1,0:T(8,128)(2,1)S(1)}, bf16[16,3,16,128]{3,2,1,0:T(8,128)(2,1)S(1)}, u32[]{:S(2)}, u32[]{:S(2)}) %collective-permute-start) | collective-permute-done | bytes 196640 | tf_op jit(solution)/shard_map/ppermute | solution.py:202
  64.0 1.8 %collective-permute-done.1.right = bf16[16,3,16,128]{3,2,1,0:T(8,128)(2,1)S(1)} collective-permute-done((bf16[16,3,16,128]{3,2,1,0:T(8,128)(2,1)S(1)}, bf16[16,3,16,128]{3,2,1,0:T(8,128)(2,1)S(1)}, u32[]{:S(2)}, u32[]{:S(2)}) %collective-permute-start.1) | collective-permute-done | bytes 196640 | tf_op jit(solution)/shard_map/ppermute | solution.py:203
  65.8 1.7 %lend.1 = (bf16[2,256,128]{2,1,0:T(8,128)(2,1)S(1)}, bf16[2,256,128]{2,1,0:T(8,128)(2,1)S(1)}) custom-call(bf16[16,3,144,128]{3,2,1,0:T(8,128)(2,1)S(1)} %all_to_all.10.own, bf16[16,3,16,128]{3,2,1,0:T(8,128)(2,1)S(1)} %collective-permute-done.left, bf16[16,3,16,128]{3,2,1,0:T(8,128)(2,1)S(1)} %collective-permute-done.1.right), custom_call_target="tpu_custom_call" | custom-call | flops 536870912 | bytes 2097152 | tf_op jit(solution)/shard_map/lend/pallas_call | solution.py:205
  67.5 8.1 %collective-permute-start.2 = (bf16[2,256,128]{2,1,0:T(8,128)(2,1)S(1)}, bf16[2,256,128]{2,1,0:T(8,128)(2,1)S(1)}, u32[]{:S(2)}, u32[]{:S(2)}) collective-permute-start(bf16[2,256,128]{2,1,0:T(8,128)(2,1)S(1)} %get-tuple-element.9), channel_id=1, source_target_pairs={{0,16},{16,32},{32,48},{48,64},{64,80},{80,96},{96,112},{112,128},... | collective-permute-start | bytes 393224 | tf_op jit(solution)/shard_map/ppermute | solution.py:215
  75.6 1.9 %collective-permute-start.3 = (bf16[2,256,128]{2,1,0:T(8,128)(2,1)S(1)}, bf16[2,256,128]{2,1,0:T(8,128)(2,1)S(1)}, u32[]{:S(2)}, u32[]{:S(2)}) collective-permute-start(bf16[2,256,128]{2,1,0:T(8,128)(2,1)S(1)} %get-tuple-element.10), channel_id=1, source_target_pairs={{16,0},{32,16},{48,32},{64,48},{80,64},{96,80},{112,96},{128,112},... | collective-permute-start | bytes 393224 | tf_op jit(solution)/shard_map/ppermute | solution.py:216
  77.5 8.8 %attend.1 = (bf16[16,144,128]{2,1,0:T(8,128)(2,1)S(1)}, f32[256,128]{1,0:T(8,128)S(1)}, f32[256,128]{1,0:T(8,128)S(1)}) custom-call(s32[32,3]{1,0:T(8,128)S(1)} %copy.7.pairs, bf16[16,3,144,128]{3,2,1,0:T(8,128)(2,1)S(1)} %all_to_all.10.own, bf16[16,3,16,128]{3,2,1,0:T(8,128)(2,1)S(1)} %collective-permute-done.left, ...), custom_call_target="tpu_custom_call" | custom-call | flops 3321888768 | bytes 3145728 | tf_op jit(solution)/shard_map/attend/pallas_call | solution.py:219
  86.4 0.0 collective-permute-done.2.from_left
  86.4 0.0 collective-permute-done.3.from_right
  86.4 1.2 %merge.1 = bf16[16,144,128]{2,1,0:T(8,128)(2,1)S(1)} custom-call(s32[32,3]{1,0:T(8,128)S(1)} %copy.7.pairs, f32[256,128]{1,0:T(8,128)S(1)} %get-tuple-element.7.audio, f32[256,128]{1,0:T(8,128)S(1)} %get-tuple-element.8.level, bf16[2,256,128]{2,1,0:T(8,128)(2,1)S(1)} %collective-permute-done.2.from_left, ...), custom_call_target="tpu_custom_call", output_to_operand_aliasing={{}: (5, {})} | custom-call | tf_op jit(solution)/shard_map/merge/pallas_call | solution.py:230
  87.6 23.2 %all_to_all.11.heads = bf16[16,144,128]{2,1,0:T(8,128)(2,1)S(1)} all-to-all(bf16[16,144,128]{2,1,0:T(8,128)(2,1)S(1)} %merge.1), channel_id=1, replica_groups=mesh['seq'=32,'head'=16] {'head'}, dimensions={0} | all-to-all | bytes 1179648 | tf_op jit(solution)/shard_map/all_to_all | solution.py:240
  110.8 1.0 unpack.1
  (1 shorter events, 0.0 us)
Async XLA Ops:
  0.6 1.4 %copy-start = (bf16[128,3,2048]{2,0,1:T(8,128)(2,1)S(1)}, bf16[128,3,2048]{2,0,1:T(8,128)(2,1)}, u32[]{:S(2)}) copy-start(bf16[128,3,2048]{2,0,1:T(8,128)(2,1)} %param.3) | copy-start | bytes 4718596
  2.0 0.9 copy-start.1
  3.3 59.3 %copy-start.2 = (s32[32,3]{0,1:T(4,128)S(1)}, s32[32,3]{0,1:T(4,128)}, u32[]{:S(2)}) copy-start(s32[32,3]{0,1:T(4,128)} %param.5) | copy-start | bytes 1156
  55.5 8.5 %collective-permute-start = (bf16[16,3,16,128]{3,2,1,0:T(8,128)(2,1)S(1)}, bf16[16,3,16,128]{3,2,1,0:T(8,128)(2,1)S(1)}, u32[]{:S(2)}, u32[]{:S(2)}) collective-permute-start(bf16[16,3,16,128]{3,2,1,0:T(8,128)(2,1)S(1)} %slice.4), channel_id=1, source_target_pairs={{0,16},{16,32},{32,48},{48,64},{64,80},{80,96},{96,112},{112,128},... | collective-permute-start | bytes 589832 | tf_op jit(solution)/shard_map/ppermute | solution.py:202
  57.5 8.3 %collective-permute-start.1 = (bf16[16,3,16,128]{3,2,1,0:T(8,128)(2,1)S(1)}, bf16[16,3,16,128]{3,2,1,0:T(8,128)(2,1)S(1)}, u32[]{:S(2)}, u32[]{:S(2)}) collective-permute-start(bf16[16,3,16,128]{3,2,1,0:T(8,128)(2,1)S(1)} %slice.4), channel_id=1, source_target_pairs={{16,0},{32,16},{48,32},{64,48},{80,64},{96,80},{112,96},{128,112},... | collective-permute-start | bytes 589832 | tf_op jit(solution)/shard_map/ppermute | solution.py:203
  67.5 18.9 %collective-permute-start.2 = (bf16[2,256,128]{2,1,0:T(8,128)(2,1)S(1)}, bf16[2,256,128]{2,1,0:T(8,128)(2,1)S(1)}, u32[]{:S(2)}, u32[]{:S(2)}) collective-permute-start(bf16[2,256,128]{2,1,0:T(8,128)(2,1)S(1)} %get-tuple-element.9), channel_id=1, source_target_pairs={{0,16},{16,32},{32,48},{48,64},{64,80},{80,96},{96,112},{112,128},... | collective-permute-start | bytes 393224 | tf_op jit(solution)/shard_map/ppermute | solution.py:215
  75.6 10.8 %collective-permute-start.3 = (bf16[2,256,128]{2,1,0:T(8,128)(2,1)S(1)}, bf16[2,256,128]{2,1,0:T(8,128)(2,1)S(1)}, u32[]{:S(2)}, u32[]{:S(2)}) collective-permute-start(bf16[2,256,128]{2,1,0:T(8,128)(2,1)S(1)} %get-tuple-element.10), channel_id=1, source_target_pairs={{16,0},{32,16},{48,32},{64,48},{80,64},{96,80},{112,96},{128,112},... | collective-permute-start | bytes 393224 | tf_op jit(solution)/shard_map/ppermute | solution.py:216

commit v2 on v1

v2 whole, which is shorter than its diff:
```python
import math

import jax
import jax.numpy as jnp
from jax import lax
from jax.experimental import pallas as pl
from jax.experimental.pallas import tpu as pltpu
from jax.sharding import PartitionSpec as P

HD = 128
PEERS = 16
BLOCKS = 32
VT, AT = 128, 16
VB, AB = PEERS * VT, PEERS * AT
KEYS = VB + 3 * AB
STEP = 256
SCALE = math.log2(math.e) / math.sqrt(HD)
VMEM_LIMIT = 32 << 20
PACK_LIMIT = 59 << 20
BF16, F32 = jnp.bfloat16, jnp.float32
ON_ROWS = (((1,), (1,)), ((), ()))


VIDEO_Q, VIDEO_K, VIDEO_V = ((c * VT, (c + 1) * VT) for c in range(3))
AUDIO_Q, AUDIO_K, AUDIO_V = ((c * AT, (c + 1) * AT) for c in range(3))


def rows(ref, span):
    return ref[:, span[0] : span[1]].reshape(-1, HD)


def stage(sources, keys, values):
    low = 0
    for ref, key_span, value_span in sources:
        part = rows(ref, key_span)
        keys[low : low + part.shape[0]] = part
        values[low : low + part.shape[0], 0:HD] = rows(ref, value_span)
        low += part.shape[0]
    values[:, HD : 2 * HD] = jnp.ones((values.shape[0], HD), BF16)


def score(queries, keys, buffer, columns, bias):
    largest = None
    for place, j in enumerate(columns):
        part = lax.dot_general(
            queries, keys[j * STEP : (j + 1) * STEP], ON_ROWS, preferred_element_type=F32
        )
        if j in bias:
            part = part + bias[j]
        buffer[:, place * STEP : (place + 1) * STEP] = part
        for t in range(0, STEP, HD):
            lanes = part[:, t : t + HD]
            largest = lanes if largest is None else jnp.maximum(largest, lanes)
    return jnp.max(largest, axis=1, keepdims=True) * SCALE


def weigh(buffer, columns, largest, values):
    low, high = columns[0] * STEP, (columns[-1] + 1) * STEP
    scores = buffer[:, 0 : high - low]
    weights = jnp.exp2(scores * SCALE - largest).astype(BF16)
    summed = jnp.dot(weights, values[low:high], preferred_element_type=F32)
    return summed[:, :HD], summed[:, HD:]


def pipelined(jobs, buffers, keys, values):
    pending = None
    for index, (load, columns, bias, finish) in enumerate(jobs):
        buffer = buffers.at[index % 2]
        largest = score(load(), keys, buffer, columns, bias)
        if pending is not None:
            pending()

        def pending(buffer=buffer, columns=columns, largest=largest, finish=finish):
            summed, total = weigh(buffer, columns, largest, values)
            finish(summed, total, largest)

    pending()


def pack_kernel(source, out, held, sems):
    cuts, _, count, _ = held.shape
    tokens = cuts * count
    copies = [
        pltpu.make_async_copy(source.at[:, i * count : (i + 1) * count], held.at[i], sems.at[i])
        for i in range(cuts)
    ]
    for copy in copies:
        copy.start()
    for i in range(cuts):
        copies[i].wait()
        for h in range(PEERS):
            for c in range(3):
                low = c * tokens + i * count
                out[h, low : low + count] = held[i, c, :, h * HD : (h + 1) * HD]


FAR_AT, MARKS_AT, NEAR_AT, OWN_AT = range(4)
FAR, NEAR, OWN = range(3)


def unpack_kernel(heads, video):
    for h in range(PEERS):
        video[:, h * HD : (h + 1) * HD] = heads[h]


def pieces(level):
    high = level.astype(BF16).astype(F32)
    middle = (level - high).astype(BF16).astype(F32)
    return high, middle, level - high - middle


def lend_kernel(own, audio, far, near, parts, keys, values, buffers, levels):
    stage([(own, VIDEO_K, VIDEO_V), (audio, AUDIO_K, AUDIO_V)], keys, values)

    def job(source, count, slot, at):
        def finish(summed, total, largest):
            parts[:, at] = (summed / total).astype(BF16).reshape(PEERS, AT, HD)
            levels[slot] = largest + jnp.log2(total)

        return (lambda: rows(source, AUDIO_Q), tuple(range(count // STEP)), {}, finish)

    jobs = [
        job(audio, VB + AB, OWN, OWN_AT),
        job(near, VB, NEAR, NEAR_AT),
        job(far, VB, FAR, FAR_AT),
    ]
    pipelined(jobs, buffers, keys, values)
    lane = lax.broadcasted_iota(jnp.int32, (AB, HD), 1)
    marks = jnp.zeros((AB, HD), F32)
    for slot in (FAR, NEAR, OWN):
        for k, piece in enumerate(pieces(levels[slot])):
            marks = jnp.where(lane == 3 * slot + k, piece, marks)
    parts[:, MARKS_AT] = marks.astype(BF16).reshape(PEERS, AT, HD)


def main_kernel(pairs, own, audio, far, near, out, keys, values, buffers):
    place = lax.axis_index("seq")
    stage([(own, VIDEO_K, VIDEO_V)] + [(a, AUDIO_K, AUDIO_V) for a in (audio, far, near)], keys, values)
    even = lax.rem(place, 2) == 0
    left, right = pairs[place, 0] == 1, pairs[place, 2] == 1
    far_valid, near_valid = jnp.where(even, left, right), jnp.where(even, right, left)
    first = VB // STEP + 1
    bias = {
        first: jnp.where(far_valid, 0.0, -jnp.inf).astype(F32),
        first + 1: jnp.where(near_valid, 0.0, -jnp.inf).astype(F32),
    }
    count = STEP // VT

    def job(i):
        low, high = i * count, (i + 1) * count

        def finish(summed, total, largest):
            result = (summed / total).astype(BF16)
            out[low:high] = result.reshape(count, VT, HD)

        def load():
            return own[low:high, 0:VT].reshape(STEP, HD)

        return (load, tuple(range(KEYS // STEP)), bias, finish)

    pipelined([job(i) for i in range(VB // STEP)], buffers, keys, values)


def merge_kernel(pairs, parts, from_far, from_near, out):
    place = lax.axis_index("seq")
    left = (place > 0) & (pairs[jnp.maximum(place - 1, 0), 2] == 1)
    right = (place < BLOCKS - 1) & (pairs[jnp.minimum(place + 1, BLOCKS - 1), 0] == 1)
    even = lax.rem(place, 2) == 0
    far_valid, near_valid = jnp.where(even, left, right), jnp.where(even, right, left)

    def level(marks, slot):
        marks = marks.astype(F32).reshape(AB, HD)
        return sum(marks[:, 3 * slot + k : 3 * slot + k + 1] for k in range(3))

    def masked(value, valid):
        return value + jnp.where(valid, 0.0, -jnp.inf).astype(F32)

    levels = [
        level(parts[:, MARKS_AT], OWN),
        masked(level(from_far[:, 1], FAR), far_valid),
        masked(level(from_near[:, 0], NEAR), near_valid),
    ]
    largest = jnp.maximum(jnp.maximum(levels[0], levels[1]), levels[2])
    shares = [jnp.exp2(l - largest) for l in levels]
    summed = jnp.zeros((AB, HD), F32)
    for share, part in zip(shares, (parts[:, OWN_AT], from_far[:, 0], from_near[:, 1])):
        summed = summed + share * part.astype(F32).reshape(AB, HD)
    result = (summed / (shares[0] + shares[1] + shares[2])).astype(BF16)
    for h in range(PEERS):
        out[:, h * HD : (h + 1) * HD] = result[h * AT : (h + 1) * AT]


IN_VMEM = pl.BlockSpec(memory_space=pltpu.VMEM)
IN_PLACE = pl.BlockSpec(memory_space=pltpu.HBM)
IN_SMEM = pl.BlockSpec(memory_space=pltpu.SMEM)


def cost(rows_, keys_, moved):
    return pl.CostEstimate(
        flops=4 * rows_ * keys_ * HD, bytes_accessed=moved, transcendentals=rows_ * keys_
    )


def scratch(keys_):
    return [
        pltpu.VMEM((keys_, HD), BF16),
        pltpu.VMEM((keys_, 2 * HD), BF16),
        pltpu.VMEM((2, STEP, keys_), F32),
    ]


def swap(block, first):
    pairs_ = [(i, i + 1) for i in range(first, BLOCKS - 1, 2)]
    return lax.ppermute(block, "seq", pairs_ + [(j, i) for i, j in pairs_])


def on_device(video_qkv, audio_qkv, pairs):
    params = pltpu.CompilerParams(vmem_limit_bytes=VMEM_LIMIT)
    video, audio = video_qkv.transpose(1, 0, 2), audio_qkv.transpose(1, 0, 2)

    def sent(source, tokens, cuts, name):
        return pl.pallas_call(
            pack_kernel,
            out_shape=jax.ShapeDtypeStruct((PEERS, 3 * tokens, HD), BF16),
            in_specs=[IN_PLACE],
            out_specs=IN_VMEM,
            scratch_shapes=[
                pltpu.VMEM((cuts, 3, tokens // cuts, PEERS * HD), BF16),
                pltpu.SemaphoreType.DMA((cuts,)),
            ],
            compiler_params=pltpu.CompilerParams(vmem_limit_bytes=PACK_LIMIT),
            cost_estimate=pl.CostEstimate(
                flops=0, bytes_accessed=tokens * 3 * PEERS * HD * 4, transcendentals=0
            ),
            name=name,
        )(source)

    def exchanged(block):
        return lax.all_to_all(block, "head", split_axis=0, concat_axis=0, tiled=True)

    own_audio = exchanged(sent(audio, AT, 1, "pack_audio"))
    own = exchanged(sent(video, VT, 4, "pack_video"))
    far = swap(own_audio, 1)
    near = swap(own_audio, 0)
    parts = pl.pallas_call(
        lend_kernel,
        out_shape=jax.ShapeDtypeStruct((PEERS, 4, AT, HD), BF16),
        in_specs=[IN_VMEM] * 4,
        out_specs=IN_VMEM,
        scratch_shapes=scratch(VB + AB) + [pltpu.VMEM((3, AB, HD), F32)],
        compiler_params=params,
        cost_estimate=cost(3 * AB, VB, 2 << 20),
        name="lend",
    )(own, own_audio, far, near)
    parts = exchanged(parts)
    out = pl.pallas_call(
        main_kernel,
        out_shape=jax.ShapeDtypeStruct((PEERS, VT, HD), BF16),
        in_specs=[IN_SMEM] + [IN_VMEM] * 4,
        out_specs=IN_VMEM,
        scratch_shapes=scratch(KEYS),
        compiler_params=params,
        cost_estimate=cost(VB, KEYS, 3 << 20),
        name="attend",
    )(pairs, own, own_audio, far, near)
    back = exchanged(out)
    from_far = swap(parts[:, FAR_AT : MARKS_AT + 1], 1)
    from_near = swap(parts[:, MARKS_AT : NEAR_AT + 1], 0)
    audio_out = pl.pallas_call(
        merge_kernel,
        out_shape=jax.ShapeDtypeStruct((AT, PEERS * HD), BF16),
        in_specs=[IN_SMEM] + [IN_VMEM] * 3,
        out_specs=IN_VMEM,
        compiler_params=params,
        name="merge",
    )(pairs, parts, from_far, from_near)
    video_out = pl.pallas_call(
        unpack_kernel,
        out_shape=jax.ShapeDtypeStruct((VT, PEERS * HD), BF16),
        in_specs=[IN_VMEM],
        out_specs=IN_VMEM,
        compiler_params=params,
        name="unpack",
    )(back)
    return video_out, audio_out


def solution(mesh):
    return jax.shard_map(
        on_device,
        mesh=mesh,
        in_specs=(P(("seq", "head"), None, None), P(("seq", "head"), None, None), P()),
        out_specs=(P(("seq", "head"), None), P(("seq", "head"), None)),
        check_vma=False,
    )
```

time: 112 us -> 105 us (0.938)
  the two profiles are of different devices: /device:TPU:196 before, /device:TPU:448 now
where the time goes in v2:
time: 105 us
  waiting for transfers between devices  50.3 us (48%)
  starting transfers between devices  34 us (32%)
  Pallas kernels  19.3 us (18%)
    all_to_all x4, waiting for transfers between devices, exchanged(): lax.all_to_all(block, 'head', split_axis=0, concat_axis=0, tiled=True)  45 us
    all_to_all x4, starting transfers between devices, exchanged(): lax.all_to_all(block, 'head', split_axis=0, concat_axis=0, tiled=True)  20.7 us
    ppermute x4, starting transfers between devices, swap(): return lax.ppermute(block, 'seq', pairs_ + [(j, i) for i, j in pairs_])  13.3 us
    pallas_call x1, Pallas kernels, on_device(): pl.pallas_call(main_kernel, out_shape=jax.ShapeDtypeStruct((PEERS, VT, HD...  8.95 us
    ppermute x4, waiting for transfers between devices, swap(): return lax.ppermute(block, 'seq', pairs_ + [(j, i) for i, j in pairs_])  5.32 us
    pallas_call x2, Pallas kernels, sent(): pl.pallas_call(pack_kernel, out_shape=jax.ShapeDtypeStruct((PEERS, 3 * to...  4.26 us
    pallas_call x1, Pallas kernels, on_device(): pl.pallas_call(lend_kernel, out_shape=jax.ShapeDtypeStruct((PEERS, 4, AT,...  3.15 us
  transfers between devices with their start and end apart: 8, of which 6 were waited for; matrix products, arithmetic and copies ran while one was open for 0% of the time, Pallas kernels for 13%

profile of v2, /device:TPU:448, one launch (start us, length us, event | category | flops | bytes accessed | tf_op | source)
XLA Modules:
  0.0 104.5 jit_solution(7175502963764234216)
XLA Ops:
  0.6 1.6 %pack_audio.1 = bf16[16,48,128]{2,1,0:T(8,128)(2,1)} custom-call(bf16[3,16,2048]{2,1,0:T(8,128)(2,1)} %bitcast.3), custom_call_target="tpu_custom_call" | custom-call | bytes 393216 | tf_op jit(solution)/shard_map/pack_audio/pallas_call | solution.py:222
  2.3 8.1 %all-to-all-start.1 = ((bf16[16,48,128]{2,1,0:T(8,128)(2,1)}), bf16[16,48,128]{2,1,0:T(8,128)(2,1)S(1)}, u32[]{:S(2)}, u32[]{:S(2)}) async-start(bf16[16,48,128]{2,1,0:T(8,128)(2,1)} %pack_audio.1), calls=%async_computation.1 | async-start | bytes 393216 | tf_op jit(solution)/shard_map/all_to_all | solution.py:239
  10.4 2.6 %pack_video.1 = bf16[16,384,128]{2,1,0:T(8,128)(2,1)} custom-call(bf16[3,128,2048]{2,1,0:T(8,128)(2,1)} %bitcast.2), custom_call_target="tpu_custom_call" | custom-call | bytes 3145728 | tf_op jit(solution)/shard_map/pack_video/pallas_call | solution.py:222
  13.1 8.3 %all-to-all-done.1.audio = bf16[16,48,128]{2,1,0:T(8,128)(2,1)S(1)} async-done(((bf16[16,48,128]{2,1,0:T(8,128)(2,1)}), bf16[16,48,128]{2,1,0:T(8,128)(2,1)S(1)}, u32[]{:S(2)}, u32[]{:S(2)}) %all-to-all-start.1) | async-done | bytes 196640 | tf_op jit(solution)/shard_map/all_to_all | solution.py:239
  21.3 3.7 %all-to-all-start = ((bf16[16,384,128]{2,1,0:T(8,128)(2,1)}), bf16[16,384,128]{2,1,0:T(8,128)(2,1)S(1)}, u32[]{:S(2)}, u32[]{:S(2)}) async-start(bf16[16,384,128]{2,1,0:T(8,128)(2,1)} %pack_video.1), calls=%async_computation | async-start | bytes 3145728 | tf_op jit(solution)/shard_map/all_to_all | solution.py:239
  25.0 0.0 copy-start
  25.0 2.2 %collective-permute-start = (bf16[16,48,128]{2,1,0:T(8,128)(2,1)S(1)}, bf16[16,48,128]{2,1,0:T(8,128)(2,1)S(1)}, u32[]{:S(2)}, u32[]{:S(2)}) collective-permute-start(bf16[16,48,128]{2,1,0:T(8,128)(2,1)S(1)} %all-to-all-done.1.audio), channel_id=1, source_target_pairs={{16,32},{48,64},{80,96},{112,128},{144,160},{176,192},{208,224},{2... | collective-permute-start | bytes 589832 | tf_op jit(solution)/shard_map/ppermute | solution.py:214
  27.2 4.5 %collective-permute-start.1 = (bf16[16,48,128]{2,1,0:T(8,128)(2,1)S(1)}, bf16[16,48,128]{2,1,0:T(8,128)(2,1)S(1)}, u32[]{:S(2)}, u32[]{:S(2)}) collective-permute-start(bf16[16,48,128]{2,1,0:T(8,128)(2,1)S(1)} %all-to-all-done.1.audio), channel_id=1, source_target_pairs={{0,16},{32,48},{64,80},{96,112},{128,144},{160,176},{192,208},{224... | collective-permute-start | bytes 589832 | tf_op jit(solution)/shard_map/ppermute | solution.py:214
  31.7 2.8 %collective-permute-done.far = bf16[16,48,128]{2,1,0:T(8,128)(2,1)S(1)} collective-permute-done((bf16[16,48,128]{2,1,0:T(8,128)(2,1)S(1)}, bf16[16,48,128]{2,1,0:T(8,128)(2,1)S(1)}, u32[]{:S(2)}, u32[]{:S(2)}) %collective-permute-start) | collective-permute-done | bytes 196640 | tf_op jit(solution)/shard_map/ppermute | solution.py:214
  34.5 0.0 collective-permute-done.1.near
  34.5 28.5 %all-to-all-done.own = bf16[16,384,128]{2,1,0:T(8,128)(2,1)S(1)} async-done(((bf16[16,384,128]{2,1,0:T(8,128)(2,1)}), bf16[16,384,128]{2,1,0:T(8,128)(2,1)S(1)}, u32[]{:S(2)}, u32[]{:S(2)}) %all-to-all-start) | async-done | bytes 1572896 | tf_op jit(solution)/shard_map/all_to_all | solution.py:239
  63.1 3.2 %lend.1 = bf16[16,4,16,128]{3,2,1,0:T(8,128)(2,1)} custom-call(bf16[16,384,128]{2,1,0:T(8,128)(2,1)S(1)} %all-to-all-done.own, bf16[16,48,128]{2,1,0:T(8,128)(2,1)S(1)} %all-to-all-done.1.audio, bf16[16,48,128]{2,1,0:T(8,128)(2,1)S(1)} %collective-permute-done.far, bf16[16,48,128]{2,1,0:T(8,128)(2,1)S(1)} %collective-permute-done.1.near), custom_call_target="tpu_custom_call" | custom-call | flops 805306368 | bytes 2097152 | tf_op jit(solution)/shard_map/lend/pallas_call | solution.py:245
  66.2 3.5 %all-to-all-start.3 = ((bf16[16,4,16,128]{3,2,1,0:T(8,128)(2,1)}), bf16[16,4,16,128]{3,2,1,0:T(8,128)(2,1)S(1)}, u32[]{:S(2)}, u32[]{:S(2)}) async-start(bf16[16,4,16,128]{3,2,1,0:T(8,128)(2,1)} %lend.1), calls=%async_computation.3 | async-start | bytes 524288 | tf_op jit(solution)/shard_map/all_to_all | solution.py:239
  69.8 0.0 copy-done
  69.8 0.1 copy.5.pairs
  69.9 9.0 %attend.1 = bf16[16,128,128]{2,1,0:T(8,128)(2,1)} custom-call(s32[32,3]{1,0:T(8,128)S(1)} %copy.5.pairs, bf16[16,384,128]{2,1,0:T(8,128)(2,1)S(1)} %all-to-all-done.own, bf16[16,48,128]{2,1,0:T(8,128)(2,1)S(1)} %all-to-all-done.1.audio, bf16[16,48,128]{2,1,0:T(8,128)(2,1)S(1)} %collective-permute-done.far, bf16[16,48,128]{2,1,0:T(8,128)(2,1)S(1)} %collective-permute-done.1.near), custom_call_target="tpu_custom_call" | custom-call | flops 2952790016 | bytes 3145728 | tf_op jit(solution)/shard_map/attend/pallas_call | solution.py:256
  78.8 2.7 %all-to-all-done.3.parts = bf16[16,4,16,128]{3,2,1,0:T(8,128)(2,1)S(1)} async-done(((bf16[16,4,16,128]{3,2,1,0:T(8,128)(2,1)}), bf16[16,4,16,128]{3,2,1,0:T(8,128)(2,1)S(1)}, u32[]{:S(2)}, u32[]{:S(2)}) %all-to-all-start.3) | async-done | bytes 262176 | tf_op jit(solution)/shard_map/all_to_all | solution.py:239
  81.5 5.3 %all-to-all-start.2 = ((bf16[16,128,128]{2,1,0:T(8,128)(2,1)}), bf16[16,128,128]{2,1,0:T(8,128)(2,1)S(1)}, u32[]{:S(2)}, u32[]{:S(2)}) async-start(bf16[16,128,128]{2,1,0:T(8,128)(2,1)} %attend.1), calls=%async_computation.2 | async-start | bytes 1048576 | tf_op jit(solution)/shard_map/all_to_all | solution.py:239
  86.9 2.9 %collective-permute-start.2 = (bf16[16,2,16,128]{3,2,1,0:T(8,128)(2,1)S(1)}, bf16[16,2,16,128]{3,2,1,0:T(8,128)(2,1)S(1)}, u32[]{:S(2)}, u32[]{:S(2)}) collective-permute-start(bf16[16,2,16,128]{3,2,1,0:T(8,128)(2,1)S(1)} %get-tuple-element.3), channel_id=1, source_target_pairs={{16,32},{48,64},{80,96},{112,128},{144,160},{176,192},{208,224},{2... | collective-permute-start | bytes 393224 | tf_op jit(solution)/shard_map/ppermute | solution.py:214
  89.8 3.7 %collective-permute-start.3 = (bf16[16,2,16,128]{3,2,1,0:T(8,128)(2,1)S(1)}, bf16[16,2,16,128]{3,2,1,0:T(8,128)(2,1)S(1)}, u32[]{:S(2)}, u32[]{:S(2)}) collective-permute-start(bf16[16,2,16,128]{3,2,1,0:T(8,128)(2,1)S(1)} %get-tuple-element.2), channel_id=1, source_target_pairs={{0,16},{32,48},{64,80},{96,112},{128,144},{160,176},{192,208},{224... | collective-permute-start | bytes 393224 | tf_op jit(solution)/shard_map/ppermute | solution.py:214
  93.6 2.5 %collective-permute-done.2.from_far = bf16[16,2,16,128]{3,2,1,0:T(8,128)(2,1)S(1)} collective-permute-done((bf16[16,2,16,128]{3,2,1,0:T(8,128)(2,1)S(1)}, bf16[16,2,16,128]{3,2,1,0:T(8,128)(2,1)S(1)}, u32[]{:S(2)}, u32[]{:S(2)}) %collective-permute-start.2) | collective-permute-done | bytes 131104 | tf_op jit(solution)/shard_map/ppermute | solution.py:214
  96.1 0.0 collective-permute-done.3.from_near
  96.1 2.0 %merge.1 = bf16[16,2048]{1,0:T(8,128)(2,1)} custom-call(s32[32,3]{1,0:T(8,128)S(1)} %copy.5.pairs, bf16[16,4,16,128]{3,2,1,0:T(8,128)(2,1)S(1)} %all-to-all-done.3.parts, bf16[16,2,16,128]{3,2,1,0:T(8,128)(2,1)S(1)} %collective-permute-done.2.from_far, bf16[16,2,16,128]{3,2,1,0:T(8,128)(2,1)S(1)} %collective-permute-done.3.from_near), custom_call_target="tpu_custom_call" | custom-call | tf_op jit(solution)/shard_map/merge/pallas_call | solution.py:269
  98.1 5.5 %all-to-all-done.2.heads = bf16[16,128,128]{2,1,0:T(8,128)(2,1)S(1)} async-done(((bf16[16,128,128]{2,1,0:T(8,128)(2,1)}), bf16[16,128,128]{2,1,0:T(8,128)(2,1)S(1)}, u32[]{:S(2)}, u32[]{:S(2)}) %all-to-all-start.2) | async-done | bytes 524320 | tf_op jit(solution)/shard_map/all_to_all | solution.py:239
  103.6 0.9 unpack.1
  (1 shorter events, 0.0 us)
Async XLA Ops:
  2.3 19.0 %all-to-all-start.1 = ((bf16[16,48,128]{2,1,0:T(8,128)(2,1)}), bf16[16,48,128]{2,1,0:T(8,128)(2,1)S(1)}, u32[]{:S(2)}, u32[]{:S(2)}) async-start(bf16[16,48,128]{2,1,0:T(8,128)(2,1)} %pack_audio.1), calls=%async_computation.1 | async-start | bytes 393216 | tf_op jit(solution)/shard_map/all_to_all | solution.py:239
  21.3 41.8 %all-to-all-start = ((bf16[16,384,128]{2,1,0:T(8,128)(2,1)}), bf16[16,384,128]{2,1,0:T(8,128)(2,1)S(1)}, u32[]{:S(2)}, u32[]{:S(2)}) async-start(bf16[16,384,128]{2,1,0:T(8,128)(2,1)} %pack_video.1), calls=%async_computation | async-start | bytes 3145728 | tf_op jit(solution)/shard_map/all_to_all | solution.py:239
  25.0 44.7 %copy-start = (s32[32,3]{0,1:T(4,128)S(1)}, s32[32,3]{0,1:T(4,128)}, u32[]{:S(2)}) copy-start(s32[32,3]{0,1:T(4,128)} %param.5) | copy-start | bytes 1156
  25.0 9.5 %collective-permute-start = (bf16[16,48,128]{2,1,0:T(8,128)(2,1)S(1)}, bf16[16,48,128]{2,1,0:T(8,128)(2,1)S(1)}, u32[]{:S(2)}, u32[]{:S(2)}) collective-permute-start(bf16[16,48,128]{2,1,0:T(8,128)(2,1)S(1)} %all-to-all-done.1.audio), channel_id=1, source_target_pairs={{16,32},{48,64},{80,96},{112,128},{144,160},{176,192},{208,224},{2... | collective-permute-start | bytes 589832 | tf_op jit(solution)/shard_map/ppermute | solution.py:214
  27.2 7.3 %collective-permute-start.1 = (bf16[16,48,128]{2,1,0:T(8,128)(2,1)S(1)}, bf16[16,48,128]{2,1,0:T(8,128)(2,1)S(1)}, u32[]{:S(2)}, u32[]{:S(2)}) collective-permute-start(bf16[16,48,128]{2,1,0:T(8,128)(2,1)S(1)} %all-to-all-done.1.audio), channel_id=1, source_target_pairs={{0,16},{32,48},{64,80},{96,112},{128,144},{160,176},{192,208},{224... | collective-permute-start | bytes 589832 | tf_op jit(solution)/shard_map/ppermute | solution.py:214
  66.2 15.3 %all-to-all-start.3 = ((bf16[16,4,16,128]{3,2,1,0:T(8,128)(2,1)}), bf16[16,4,16,128]{3,2,1,0:T(8,128)(2,1)S(1)}, u32[]{:S(2)}, u32[]{:S(2)}) async-start(bf16[16,4,16,128]{3,2,1,0:T(8,128)(2,1)} %lend.1), calls=%async_computation.3 | async-start | bytes 524288 | tf_op jit(solution)/shard_map/all_to_all | solution.py:239
  81.5 22.1 %all-to-all-start.2 = ((bf16[16,128,128]{2,1,0:T(8,128)(2,1)}), bf16[16,128,128]{2,1,0:T(8,128)(2,1)S(1)}, u32[]{:S(2)}, u32[]{:S(2)}) async-start(bf16[16,128,128]{2,1,0:T(8,128)(2,1)} %attend.1), calls=%async_computation.2 | async-start | bytes 1048576 | tf_op jit(solution)/shard_map/all_to_all | solution.py:239
  86.9 9.2 %collective-permute-start.2 = (bf16[16,2,16,128]{3,2,1,0:T(8,128)(2,1)S(1)}, bf16[16,2,16,128]{3,2,1,0:T(8,128)(2,1)S(1)}, u32[]{:S(2)}, u32[]{:S(2)}) collective-permute-start(bf16[16,2,16,128]{3,2,1,0:T(8,128)(2,1)S(1)} %get-tuple-element.3), channel_id=1, source_target_pairs={{16,32},{48,64},{80,96},{112,128},{144,160},{176,192},{208,224},{2... | collective-permute-start | bytes 393224 | tf_op jit(solution)/shard_map/ppermute | solution.py:214
  89.8 6.2 %collective-permute-start.3 = (bf16[16,2,16,128]{3,2,1,0:T(8,128)(2,1)S(1)}, bf16[16,2,16,128]{3,2,1,0:T(8,128)(2,1)S(1)}, u32[]{:S(2)}, u32[]{:S(2)}) collective-permute-start(bf16[16,2,16,128]{3,2,1,0:T(8,128)(2,1)S(1)} %get-tuple-element.2), channel_id=1, source_target_pairs={{0,16},{32,48},{64,80},{96,112},{128,144},{160,176},{192,208},{224... | collective-permute-start | bytes 393224 | tf_op jit(solution)/shard_map/ppermute | solution.py:214

commit v3 on v2

--- a/solution.py
+++ b/solution.py
@@ -98,9 +98,18 @@
 FAR, NEAR, OWN = range(3)
 
 
-def unpack_kernel(heads, video):
-    for h in range(PEERS):
-        video[:, h * HD : (h + 1) * HD] = heads[h]
+def unpack_kernel(heads, video, held, sems):
+    cuts, count, _ = held.shape
+    copies = [
+        pltpu.make_async_copy(held.at[i], video.at[i * count : (i + 1) * count], sems.at[i])
+        for i in range(cuts)
+    ]
+    for i in range(cuts):
+        for h in range(PEERS):
+            held[i, :, h * HD : (h + 1) * HD] = heads[h, i * count : (i + 1) * count]
+        copies[i].start()
+    for copy in copies:
+        copy.wait()
 
 
 def pieces(level):
@@ -109,12 +118,14 @@
     return high, middle, level - high - middle
 
 
-def lend_kernel(own, audio, far, near, parts, keys, values, buffers, levels):
+def lend_kernel(own, audio, far, near, out, keys, values, buffers, levels, parts, sems):
     stage([(own, VIDEO_K, VIDEO_V), (audio, AUDIO_K, AUDIO_V)], keys, values)
+    copies = [pltpu.make_async_copy(parts.at[i], out.at[:, i], sems.at[i]) for i in range(4)]
 
     def job(source, count, slot, at):
         def finish(summed, total, largest):
-            parts[:, at] = (summed / total).astype(BF16).reshape(PEERS, AT, HD)
+            parts[at] = (summed / total).astype(BF16).reshape(PEERS, AT, HD)
+            copies[at].start()
             levels[slot] = largest + jnp.log2(total)
 
         return (lambda: rows(source, AUDIO_Q), tuple(range(count // STEP)), {}, finish)
@@ -130,10 +141,13 @@
     for slot in (FAR, NEAR, OWN):
         for k, piece in enumerate(pieces(levels[slot])):
             marks = jnp.where(lane == 3 * slot + k, piece, marks)
-    parts[:, MARKS_AT] = marks.astype(BF16).reshape(PEERS, AT, HD)
-
-
-def main_kernel(pairs, own, audio, far, near, out, keys, values, buffers):
+    parts[MARKS_AT] = marks.astype(BF16).reshape(PEERS, AT, HD)
+    copies[MARKS_AT].start()
+    for copy in copies:
+        copy.wait()
+
+
+def main_kernel(pairs, own, audio, far, near, out, keys, values, buffers, held, sems):
     place = lax.axis_index("seq")
     stage([(own, VIDEO_K, VIDEO_V)] + [(a, AUDIO_K, AUDIO_V) for a in (audio, far, near)], keys, values)
     even = lax.rem(place, 2) == 0
@@ -150,15 +164,24 @@
         low, high = i * count, (i + 1) * count
 
         def finish(summed, total, largest):
-            result = (summed / total).astype(BF16)
-            out[low:high] = result.reshape(count, VT, HD)
+            held[low:high] = (summed / total).astype(BF16).reshape(count, VT, HD)
+            copies[i].start()
 
         def load():
             return own[low:high, 0:VT].reshape(STEP, HD)
 
         return (load, tuple(range(KEYS // STEP)), bias, finish)
 
-    pipelined([job(i) for i in range(VB // STEP)], buffers, keys, values)
+    steps = range(VB // STEP)
+    copies = [
+        pltpu.make_async_copy(
+            held.at[i * count : (i + 1) * count], out.at[i * count : (i + 1) * count], sems.at[i]
+        )
+        for i in steps
+    ]
+    pipelined([job(i) for i in steps], buffers, keys, values)
+    for copy in copies:
+        copy.wait()
 
 
 def merge_kernel(pairs, parts, from_far, from_near, out):
@@ -168,9 +191,12 @@
     even = lax.rem(place, 2) == 0
     far_valid, near_valid = jnp.where(even, left, right), jnp.where(even, right, left)
 
+    row = lax.broadcasted_iota(jnp.int32, (HD, HD), 0)
+
     def level(marks, slot):
-        marks = marks.astype(F32).reshape(AB, HD)
-        return sum(marks[:, 3 * slot + k : 3 * slot + k + 1] for k in range(3))
+        wanted = (row >= 3 * slot) & (row < 3 * slot + 3)
+        chosen = jnp.where(wanted, 1.0, 0.0).astype(BF16)
+        return jnp.dot(marks.reshape(AB, HD), chosen, preferred_element_type=F32)
 
     def masked(value, valid):
         return value + jnp.where(valid, 0.0, -jnp.inf).astype(F32)
@@ -216,38 +242,42 @@
 
 def on_device(video_qkv, audio_qkv, pairs):
     params = pltpu.CompilerParams(vmem_limit_bytes=VMEM_LIMIT)
-    video, audio = video_qkv.transpose(1, 0, 2), audio_qkv.transpose(1, 0, 2)
-
-    def sent(source, tokens, cuts, name):
-        return pl.pallas_call(
-            pack_kernel,
-            out_shape=jax.ShapeDtypeStruct((PEERS, 3 * tokens, HD), BF16),
-            in_specs=[IN_PLACE],
-            out_specs=IN_VMEM,
-            scratch_shapes=[
-                pltpu.VMEM((cuts, 3, tokens // cuts, PEERS * HD), BF16),
-                pltpu.SemaphoreType.DMA((cuts,)),
-            ],
-            compiler_params=pltpu.CompilerParams(vmem_limit_bytes=PACK_LIMIT),
-            cost_estimate=pl.CostEstimate(
-                flops=0, bytes_accessed=tokens * 3 * PEERS * HD * 4, transcendentals=0
-            ),
-            name=name,
-        )(source)
+    pack_params = pltpu.CompilerParams(vmem_limit_bytes=PACK_LIMIT)
+
+    cuts = 4
+    packed_video = pl.pallas_call(
+        pack_kernel,
+        out_shape=jax.ShapeDtypeStruct((PEERS, 3 * VT, HD), BF16),
+        in_specs=[IN_PLACE],
+        out_specs=IN_VMEM,
+        scratch_shapes=[
+            pltpu.VMEM((cuts, 3, VT // cuts, PEERS * HD), BF16),
+            pltpu.SemaphoreType.DMA((cuts,)),
+        ],
+        compiler_params=pack_params,
+        cost_estimate=pl.CostEstimate(flops=0, bytes_accessed=4 << 20, transcendentals=0),
+        name="pack_video",
+    )(video_qkv.transpose(1, 0, 2))
 
     def exchanged(block):
         return lax.all_to_all(block, "head", split_axis=0, concat_axis=0, tiled=True)
 
-    own_audio = exchanged(sent(audio, AT, 1, "pack_audio"))
-    own = exchanged(sent(video, VT, 4, "pack_video"))
+    turned = audio_qkv.reshape(AT, 3, PEERS, HD).transpose(2, 1, 0, 3)
+    own_audio = exchanged(turned.reshape(PEERS, 3 * AT, HD))
+    own = exchanged(packed_video)
     far = swap(own_audio, 1)
     near = swap(own_audio, 0)
     parts = pl.pallas_call(
         lend_kernel,
         out_shape=jax.ShapeDtypeStruct((PEERS, 4, AT, HD), BF16),
         in_specs=[IN_VMEM] * 4,
-        out_specs=IN_VMEM,
-        scratch_shapes=scratch(VB + AB) + [pltpu.VMEM((3, AB, HD), F32)],
+        out_specs=IN_PLACE,
+        scratch_shapes=scratch(VB + AB)
+        + [
+            pltpu.VMEM((3, AB, HD), F32),
+            pltpu.VMEM((4, PEERS, AT, HD), BF16),
+            pltpu.SemaphoreType.DMA((4,)),
+        ],
         compiler_params=params,
         cost_estimate=cost(3 * AB, VB, 2 << 20),
         name="lend",
@@ -257,8 +287,9 @@
         main_kernel,
         out_shape=jax.ShapeDtypeStruct((PEERS, VT, HD), BF16),
         in_specs=[IN_SMEM] + [IN_VMEM] * 4,
-        out_specs=IN_VMEM,
-        scratch_shapes=scratch(KEYS),
+        out_specs=IN_PLACE,
+        scratch_shapes=scratch(KEYS)
+        + [pltpu.VMEM((PEERS, VT, HD), BF16), pltpu.SemaphoreType.DMA((VB // STEP,))],
         compiler_params=params,
         cost_estimate=cost(VB, KEYS, 3 << 20),
         name="attend",
@@ -278,7 +309,11 @@
         unpack_kernel,
         out_shape=jax.ShapeDtypeStruct((VT, PEERS * HD), BF16),
         in_specs=[IN_VMEM],
-        out_specs=IN_VMEM,
+        out_specs=IN_PLACE,
+        scratch_shapes=[
+            pltpu.VMEM((4, VT // 4, PEERS * HD), BF16),
+            pltpu.SemaphoreType.DMA((4,)),
+        ],
         compiler_params=params,
         name="unpack",
     )(back)

time: 105 us -> 105 us (level)
  Pallas kernels: 19.3 us -> 17.2 us
  local copies, waits for them, and re-layouts: 0.12 us -> 1.76 us
    pallas_call x2 -> x1, Pallas kernels: 4.26 us -> 2.63 us  [on_device(): pl.pallas_call(pack_kernel, out_shape=jax.ShapeDtypeStruct((PEERS, 3 * VT...]
where the time goes in v3:
time: 105 us; the launch traced here: 104 us
  waiting for transfers between devices  50.7 us (48%)
  starting transfers between devices  34 us (32%)
  Pallas kernels  17.2 us (16%)
  local copies, waits for them, and re-layouts  1.76 us (2%)
    all_to_all x4, waiting for transfers between devices, exchanged(): lax.all_to_all(block, 'head', split_axis=0, concat_axis=0, tiled=True)  45.4 us
    all_to_all x4, starting transfers between devices, exchanged(): lax.all_to_all(block, 'head', split_axis=0, concat_axis=0, tiled=True)  20.7 us
    ppermute x4, starting transfers between devices, swap(): return lax.ppermute(block, 'seq', pairs_ + [(j, i) for i, j in pairs_])  13.3 us
    pallas_call x1, Pallas kernels, on_device(): pl.pallas_call(main_kernel, out_shape=jax.ShapeDtypeStruct((PEERS, VT, HD...  8.89 us
    ppermute x4, waiting for transfers between devices, swap(): return lax.ppermute(block, 'seq', pairs_ + [(j, i) for i, j in pairs_])  5.32 us
    pallas_call x1, Pallas kernels, on_device(): pl.pallas_call(lend_kernel, out_shape=jax.ShapeDtypeStruct((PEERS, 4, AT,...  3.19 us
    pallas_call x1, Pallas kernels, on_device(): pl.pallas_call(pack_kernel, out_shape=jax.ShapeDtypeStruct((PEERS, 3 * VT...  2.63 us
  transfers between devices with their start and end apart: 8, of which 6 were waited for; matrix products, arithmetic and copies ran while one was open for 0% of the time, Pallas kernels for 13%

profile of v3, /device:TPU:448, one launch (start us, length us, event | category | flops | bytes accessed | tf_op | source)
XLA Modules:
  0.0 104.4 jit_solution(17683334536307759461)
XLA Ops:
  0.6 0.0 copy-start
  0.6 0.9 copy-done
  1.6 0.7 copy_bitcast_fusion
  2.3 8.1 %all-to-all-start.1 = ((bf16[16,48,128]{2,1,0:T(8,128)(2,1)}), bf16[16,48,128]{2,1,0:T(8,128)(2,1)S(1)}, u32[]{:S(2)}, u32[]{:S(2)}) async-start(bf16[16,48,128]{2,1,0:T(8,128)(2,1)} %bitcast.2), calls=%async_computation.1 | async-start | bytes 393216 | tf_op jit(solution)/shard_map/all_to_all | solution.py:263
  10.4 2.6 %pack_video.1 = bf16[16,384,128]{2,1,0:T(8,128)(2,1)} custom-call(bf16[3,128,2048]{2,1,0:T(8,128)(2,1)} %bitcast.9), custom_call_target="tpu_custom_call" | custom-call | bytes 4194304 | tf_op jit(solution)/shard_map/pack_video/pallas_call | solution.py:248
  13.0 8.2 %all-to-all-done.1.audio = bf16[16,48,128]{2,1,0:T(8,128)(2,1)S(1)} async-done(((bf16[16,48,128]{2,1,0:T(8,128)(2,1)}), bf16[16,48,128]{2,1,0:T(8,128)(2,1)S(1)}, u32[]{:S(2)}, u32[]{:S(2)}) %all-to-all-start.1) | async-done | bytes 196640 | tf_op jit(solution)/shard_map/all_to_all | solution.py:263
  21.3 3.7 %all-to-all-start = ((bf16[16,384,128]{2,1,0:T(8,128)(2,1)}), bf16[16,384,128]{2,1,0:T(8,128)(2,1)S(1)}, u32[]{:S(2)}, u32[]{:S(2)}) async-start(bf16[16,384,128]{2,1,0:T(8,128)(2,1)} %pack_video.1), calls=%async_computation | async-start | bytes 3145728 | tf_op jit(solution)/shard_map/all_to_all | solution.py:263
  25.0 0.0 copy-start.1
  25.0 2.2 %collective-permute-start = (bf16[16,48,128]{2,1,0:T(8,128)(2,1)S(1)}, bf16[16,48,128]{2,1,0:T(8,128)(2,1)S(1)}, u32[]{:S(2)}, u32[]{:S(2)}) collective-permute-start(bf16[16,48,128]{2,1,0:T(8,128)(2,1)S(1)} %all-to-all-done.1.audio), channel_id=1, source_target_pairs={{16,32},{48,64},{80,96},{112,128},{144,160},{176,192},{208,224},{2... | collective-permute-start | bytes 589832 | tf_op jit(solution)/shard_map/ppermute | solution.py:240
  27.2 4.5 %collective-permute-start.1 = (bf16[16,48,128]{2,1,0:T(8,128)(2,1)S(1)}, bf16[16,48,128]{2,1,0:T(8,128)(2,1)S(1)}, u32[]{:S(2)}, u32[]{:S(2)}) collective-permute-start(bf16[16,48,128]{2,1,0:T(8,128)(2,1)S(1)} %all-to-all-done.1.audio), channel_id=1, source_target_pairs={{0,16},{32,48},{64,80},{96,112},{128,144},{160,176},{192,208},{224... | collective-permute-start | bytes 589832 | tf_op jit(solution)/shard_map/ppermute | solution.py:240
  31.7 2.8 %collective-permute-done.far = bf16[16,48,128]{2,1,0:T(8,128)(2,1)S(1)} collective-permute-done((bf16[16,48,128]{2,1,0:T(8,128)(2,1)S(1)}, bf16[16,48,128]{2,1,0:T(8,128)(2,1)S(1)}, u32[]{:S(2)}, u32[]{:S(2)}) %collective-permute-start) | collective-permute-done | bytes 196640 | tf_op jit(solution)/shard_map/ppermute | solution.py:240
  34.5 0.0 collective-permute-done.1.near
  34.5 28.5 %all-to-all-done.own = bf16[16,384,128]{2,1,0:T(8,128)(2,1)S(1)} async-done(((bf16[16,384,128]{2,1,0:T(8,128)(2,1)}), bf16[16,384,128]{2,1,0:T(8,128)(2,1)S(1)}, u32[]{:S(2)}, u32[]{:S(2)}) %all-to-all-start) | async-done | bytes 1572896 | tf_op jit(solution)/shard_map/all_to_all | solution.py:263
  63.0 3.2 %lend.1 = bf16[16,4,16,128]{3,2,1,0:T(8,128)(2,1)} custom-call(bf16[16,384,128]{2,1,0:T(8,128)(2,1)S(1)} %all-to-all-done.own, bf16[16,48,128]{2,1,0:T(8,128)(2,1)S(1)} %all-to-all-done.1.audio, bf16[16,48,128]{2,1,0:T(8,128)(2,1)S(1)} %collective-permute-done.far, bf16[16,48,128]{2,1,0:T(8,128)(2,1)S(1)} %collective-permute-done.1.near), custom_call_target="tpu_custom_call" | custom-call | flops 805306368 | bytes 2097152 | tf_op jit(solution)/shard_map/lend/pallas_call | solution.py:270
  66.2 3.5 %all-to-all-start.3 = ((bf16[16,4,16,128]{3,2,1,0:T(8,128)(2,1)}), bf16[16,4,16,128]{3,2,1,0:T(8,128)(2,1)S(1)}, u32[]{:S(2)}, u32[]{:S(2)}) async-start(bf16[16,4,16,128]{3,2,1,0:T(8,128)(2,1)} %lend.1), calls=%async_computation.3 | async-start | bytes 524288 | tf_op jit(solution)/shard_map/all_to_all | solution.py:263
  69.8 0.0 copy-done.1
  69.8 0.1 copy.6.pairs
  69.9 8.9 %attend.1 = bf16[16,128,128]{2,1,0:T(8,128)(2,1)} custom-call(s32[32,3]{1,0:T(8,128)S(1)} %copy.6.pairs, bf16[16,384,128]{2,1,0:T(8,128)(2,1)S(1)} %all-to-all-done.own, bf16[16,48,128]{2,1,0:T(8,128)(2,1)S(1)} %all-to-all-done.1.audio, bf16[16,48,128]{2,1,0:T(8,128)(2,1)S(1)} %collective-permute-done.far, bf16[16,48,128]{2,1,0:T(8,128)(2,1)S(1)} %collective-permute-done.1.near), custom_call_target="tpu_custom_call" | custom-call | flops 2952790016 | bytes 3145728 | tf_op jit(solution)/shard_map/attend/pallas_call | solution.py:286
  78.8 2.8 %all-to-all-done.3.parts = bf16[16,4,16,128]{3,2,1,0:T(8,128)(2,1)S(1)} async-done(((bf16[16,4,16,128]{3,2,1,0:T(8,128)(2,1)}), bf16[16,4,16,128]{3,2,1,0:T(8,128)(2,1)S(1)}, u32[]{:S(2)}, u32[]{:S(2)}) %all-to-all-start.3) | async-done | bytes 262176 | tf_op jit(solution)/shard_map/all_to_all | solution.py:263
  81.6 5.3 %all-to-all-start.2 = ((bf16[16,128,128]{2,1,0:T(8,128)(2,1)}), bf16[16,128,128]{2,1,0:T(8,128)(2,1)S(1)}, u32[]{:S(2)}, u32[]{:S(2)}) async-start(bf16[16,128,128]{2,1,0:T(8,128)(2,1)} %attend.1), calls=%async_computation.2 | async-start | bytes 1048576 | tf_op jit(solution)/shard_map/all_to_all | solution.py:263
  86.9 2.9 %collective-permute-start.2 = (bf16[16,2,16,128]{3,2,1,0:T(8,128)(2,1)S(1)}, bf16[16,2,16,128]{3,2,1,0:T(8,128)(2,1)S(1)}, u32[]{:S(2)}, u32[]{:S(2)}) collective-permute-start(bf16[16,2,16,128]{3,2,1,0:T(8,128)(2,1)S(1)} %get-tuple-element.3), channel_id=1, source_target_pairs={{16,32},{48,64},{80,96},{112,128},{144,160},{176,192},{208,224},{2... | collective-permute-start | bytes 393224 | tf_op jit(solution)/shard_map/ppermute | solution.py:240
  89.8 3.7 %collective-permute-start.3 = (bf16[16,2,16,128]{3,2,1,0:T(8,128)(2,1)S(1)}, bf16[16,2,16,128]{3,2,1,0:T(8,128)(2,1)S(1)}, u32[]{:S(2)}, u32[]{:S(2)}) collective-permute-start(bf16[16,2,16,128]{3,2,1,0:T(8,128)(2,1)S(1)} %get-tuple-element.2), channel_id=1, source_target_pairs={{0,16},{32,48},{64,80},{96,112},{128,144},{160,176},{192,208},{224... | collective-permute-start | bytes 393224 | tf_op jit(solution)/shard_map/ppermute | solution.py:240
  93.6 2.5 %collective-permute-done.2.from_far = bf16[16,2,16,128]{3,2,1,0:T(8,128)(2,1)S(1)} collective-permute-done((bf16[16,2,16,128]{3,2,1,0:T(8,128)(2,1)S(1)}, bf16[16,2,16,128]{3,2,1,0:T(8,128)(2,1)S(1)}, u32[]{:S(2)}, u32[]{:S(2)}) %collective-permute-start.2) | collective-permute-done | bytes 131104 | tf_op jit(solution)/shard_map/ppermute | solution.py:240
  96.1 0.0 collective-permute-done.3.from_near
  96.1 1.7 %merge.1 = bf16[16,2048]{1,0:T(8,128)(2,1)} custom-call(s32[32,3]{1,0:T(8,128)S(1)} %copy.6.pairs, bf16[16,4,16,128]{3,2,1,0:T(8,128)(2,1)S(1)} %all-to-all-done.3.parts, bf16[16,2,16,128]{3,2,1,0:T(8,128)(2,1)S(1)} %collective-permute-done.2.from_far, bf16[16,2,16,128]{3,2,1,0:T(8,128)(2,1)S(1)} %collective-permute-done.3.from_near), custom_call_target="tpu_custom_call" | custom-call | tf_op jit(solution)/shard_map/merge/pallas_call | solution.py:300
  97.8 5.8 %all-to-all-done.2.heads = bf16[16,128,128]{2,1,0:T(8,128)(2,1)S(1)} async-done(((bf16[16,128,128]{2,1,0:T(8,128)(2,1)}), bf16[16,128,128]{2,1,0:T(8,128)(2,1)S(1)}, u32[]{:S(2)}, u32[]{:S(2)}) %all-to-all-start.2) | async-done | bytes 524320 | tf_op jit(solution)/shard_map/all_to_all | solution.py:263
  103.6 0.8 unpack.1
  (1 shorter events, 0.0 us)
Async XLA Ops:
  0.6 0.9 copy-start
  2.3 19.0 %all-to-all-start.1 = ((bf16[16,48,128]{2,1,0:T(8,128)(2,1)}), bf16[16,48,128]{2,1,0:T(8,128)(2,1)S(1)}, u32[]{:S(2)}, u32[]{:S(2)}) async-start(bf16[16,48,128]{2,1,0:T(8,128)(2,1)} %bitcast.2), calls=%async_computation.1 | async-start | bytes 393216 | tf_op jit(solution)/shard_map/all_to_all | solution.py:263
  21.3 41.8 %all-to-all-start = ((bf16[16,384,128]{2,1,0:T(8,128)(2,1)}), bf16[16,384,128]{2,1,0:T(8,128)(2,1)S(1)}, u32[]{:S(2)}, u32[]{:S(2)}) async-start(bf16[16,384,128]{2,1,0:T(8,128)(2,1)} %pack_video.1), calls=%async_computation | async-start | bytes 3145728 | tf_op jit(solution)/shard_map/all_to_all | solution.py:263
  25.0 44.8 %copy-start.1 = (s32[32,3]{0,1:T(4,128)S(1)}, s32[32,3]{0,1:T(4,128)}, u32[]{:S(2)}) copy-start(s32[32,3]{0,1:T(4,128)} %param.5) | copy-start | bytes 1156
  25.0 9.5 %collective-permute-start = (bf16[16,48,128]{2,1,0:T(8,128)(2,1)S(1)}, bf16[16,48,128]{2,1,0:T(8,128)(2,1)S(1)}, u32[]{:S(2)}, u32[]{:S(2)}) collective-permute-start(bf16[16,48,128]{2,1,0:T(8,128)(2,1)S(1)} %all-to-all-done.1.audio), channel_id=1, source_target_pairs={{16,32},{48,64},{80,96},{112,128},{144,160},{176,192},{208,224},{2... | collective-permute-start | bytes 589832 | tf_op jit(solution)/shard_map/ppermute | solution.py:240
  27.2 7.3 %collective-permute-start.1 = (bf16[16,48,128]{2,1,0:T(8,128)(2,1)S(1)}, bf16[16,48,128]{2,1,0:T(8,128)(2,1)S(1)}, u32[]{:S(2)}, u32[]{:S(2)}) collective-permute-start(bf16[16,48,128]{2,1,0:T(8,128)(2,1)S(1)} %all-to-all-done.1.audio), channel_id=1, source_target_pairs={{0,16},{32,48},{64,80},{96,112},{128,144},{160,176},{192,208},{224... | collective-permute-start | bytes 589832 | tf_op jit(solution)/shard_map/ppermute | solution.py:240
  66.2 15.3 %all-to-all-start.3 = ((bf16[16,4,16,128]{3,2,1,0:T(8,128)(2,1)}), bf16[16,4,16,128]{3,2,1,0:T(8,128)(2,1)S(1)}, u32[]{:S(2)}, u32[]{:S(2)}) async-start(bf16[16,4,16,128]{3,2,1,0:T(8,128)(2,1)} %lend.1), calls=%async_computation.3 | async-start | bytes 524288 | tf_op jit(solution)/shard_map/all_to_all | solution.py:263
  81.6 22.0 %all-to-all-start.2 = ((bf16[16,128,128]{2,1,0:T(8,128)(2,1)}), bf16[16,128,128]{2,1,0:T(8,128)(2,1)S(1)}, u32[]{:S(2)}, u32[]{:S(2)}) async-start(bf16[16,128,128]{2,1,0:T(8,128)(2,1)} %attend.1), calls=%async_computation.2 | async-start | bytes 1048576 | tf_op jit(solution)/shard_map/all_to_all | solution.py:263
  86.9 9.2 %collective-permute-start.2 = (bf16[16,2,16,128]{3,2,1,0:T(8,128)(2,1)S(1)}, bf16[16,2,16,128]{3,2,1,0:T(8,128)(2,1)S(1)}, u32[]{:S(2)}, u32[]{:S(2)}) collective-permute-start(bf16[16,2,16,128]{3,2,1,0:T(8,128)(2,1)S(1)} %get-tuple-element.3), channel_id=1, source_target_pairs={{16,32},{48,64},{80,96},{112,128},{144,160},{176,192},{208,224},{2... | collective-permute-start | bytes 393224 | tf_op jit(solution)/shard_map/ppermute | solution.py:240
  89.8 6.2 %collective-permute-start.3 = (bf16[16,2,16,128]{3,2,1,0:T(8,128)(2,1)S(1)}, bf16[16,2,16,128]{3,2,1,0:T(8,128)(2,1)S(1)}, u32[]{:S(2)}, u32[]{:S(2)}) collective-permute-start(bf16[16,2,16,128]{3,2,1,0:T(8,128)(2,1)S(1)} %get-tuple-element.2), channel_id=1, source_target_pairs={{0,16},{32,48},{64,80},{96,112},{128,144},{160,176},{192,208},{224... | collective-permute-start | bytes 393224 | tf_op jit(solution)/shard_map/ppermute | solution.py:240

commit v4 on v3

--- a/solution.py
+++ b/solution.py
@@ -32,18 +32,27 @@
 def stage(sources, keys, values):
     low = 0
     for ref, key_span, value_span in sources:
-        part = rows(ref, key_span)
-        keys[low : low + part.shape[0]] = part
-        values[low : low + part.shape[0], 0:HD] = rows(ref, value_span)
+        part = rows(ref, value_span)
+        values[low : low + part.shape[0], 0:HD] = part
+        if low >= VB:
+            keys[low - VB : low - VB + part.shape[0]] = rows(ref, key_span)
         low += part.shape[0]
     values[:, HD : 2 * HD] = jnp.ones((values.shape[0], HD), BF16)
+
+
+def key_step(own, keys, j):
+    video = VB // STEP
+    if j >= video:
+        return keys[(j - video) * STEP : (j - video + 1) * STEP]
+    count = STEP // VT
+    return own[j * count : (j + 1) * count, VIDEO_K[0] : VIDEO_K[1]].reshape(STEP, HD)
 
 
 def score(queries, keys, buffer, columns, bias):
     largest = None
     for place, j in enumerate(columns):
         part = lax.dot_general(
-            queries, keys[j * STEP : (j + 1) * STEP], ON_ROWS, preferred_element_type=F32
+            queries, key_step(*keys, j), ON_ROWS, preferred_element_type=F32
         )
         if j in bias:
             part = part + bias[j]
@@ -135,7 +144,7 @@
         job(near, VB, NEAR, NEAR_AT),
         job(far, VB, FAR, FAR_AT),
     ]
-    pipelined(jobs, buffers, keys, values)
+    pipelined(jobs, buffers, (own, keys), values)
     lane = lax.broadcasted_iota(jnp.int32, (AB, HD), 1)
     marks = jnp.zeros((AB, HD), F32)
     for slot in (FAR, NEAR, OWN):
@@ -179,7 +188,7 @@
         )
         for i in steps
     ]
-    pipelined([job(i) for i in steps], buffers, keys, values)
+    pipelined([job(i) for i in steps], buffers, (own, keys), values)
     for copy in copies:
         copy.wait()
 
@@ -229,7 +238,7 @@
 
 def scratch(keys_):
     return [
-        pltpu.VMEM((keys_, HD), BF16),
+        pltpu.VMEM((keys_ - VB, HD), BF16),
         pltpu.VMEM((keys_, 2 * HD), BF16),
         pltpu.VMEM((2, STEP, keys_), F32),
     ]

time: 105 us -> 105 us (level)
  no operation moved by 1% of the time
where the time goes in v4:
time: 105 us; the launch traced here: 104 us
  waiting for transfers between devices  50.7 us (48%)
  starting transfers between devices  34 us (32%)
  Pallas kernels  17.2 us (16%)
  local copies, waits for them, and re-layouts  1.76 us (2%)
    all_to_all x4, waiting for transfers between devices, exchanged(): lax.all_to_all(block, 'head', split_axis=0, concat_axis=0, tiled=True)  45.4 us
    all_to_all x4, starting transfers between devices, exchanged(): lax.all_to_all(block, 'head', split_axis=0, concat_axis=0, tiled=True)  20.6 us
    ppermute x4, starting transfers between devices, swap(): return lax.ppermute(block, 'seq', pairs_ + [(j, i) for i, j in pairs_])  13.3 us
    pallas_call x1, Pallas kernels, on_device(): pl.pallas_call(main_kernel, out_shape=jax.ShapeDtypeStruct((PEERS, VT, HD...  8.87 us
    ppermute x4, waiting for transfers between devices, swap(): return lax.ppermute(block, 'seq', pairs_ + [(j, i) for i, j in pairs_])  5.32 us
    pallas_call x1, Pallas kernels, on_device(): pl.pallas_call(lend_kernel, out_shape=jax.ShapeDtypeStruct((PEERS, 4, AT,...  3.17 us
    pallas_call x1, Pallas kernels, on_device(): pl.pallas_call(pack_kernel, out_shape=jax.ShapeDtypeStruct((PEERS, 3 * VT...  2.63 us
  transfers between devices with their start and end apart: 8, of which 6 were waited for; matrix products, arithmetic and copies ran while one was open for 0% of the time, Pallas kernels for 13%

profile of v4, /device:TPU:448, one launch (start us, length us, event | category | flops | bytes accessed | tf_op | source)
XLA Modules:
  0.0 104.4 jit_solution(9099068554766131677)
XLA Ops:
  0.6 0.0 copy-start
  0.6 0.9 copy-done
  1.6 0.7 copy_bitcast_fusion
  2.3 8.1 %all-to-all-start.1 = ((bf16[16,48,128]{2,1,0:T(8,128)(2,1)}), bf16[16,48,128]{2,1,0:T(8,128)(2,1)S(1)}, u32[]{:S(2)}, u32[]{:S(2)}) async-start(bf16[16,48,128]{2,1,0:T(8,128)(2,1)} %bitcast.2), calls=%async_computation.1 | async-start | bytes 393216 | tf_op jit(solution)/shard_map/all_to_all | solution.py:272
  10.4 2.6 %pack_video.1 = bf16[16,384,128]{2,1,0:T(8,128)(2,1)} custom-call(bf16[3,128,2048]{2,1,0:T(8,128)(2,1)} %bitcast.9), custom_call_target="tpu_custom_call" | custom-call | bytes 4194304 | tf_op jit(solution)/shard_map/pack_video/pallas_call | solution.py:257
  13.0 8.2 %all-to-all-done.1.audio = bf16[16,48,128]{2,1,0:T(8,128)(2,1)S(1)} async-done(((bf16[16,48,128]{2,1,0:T(8,128)(2,1)}), bf16[16,48,128]{2,1,0:T(8,128)(2,1)S(1)}, u32[]{:S(2)}, u32[]{:S(2)}) %all-to-all-start.1) | async-done | bytes 196640 | tf_op jit(solution)/shard_map/all_to_all | solution.py:272
  21.3 3.7 %all-to-all-start = ((bf16[16,384,128]{2,1,0:T(8,128)(2,1)}), bf16[16,384,128]{2,1,0:T(8,128)(2,1)S(1)}, u32[]{:S(2)}, u32[]{:S(2)}) async-start(bf16[16,384,128]{2,1,0:T(8,128)(2,1)} %pack_video.1), calls=%async_computation | async-start | bytes 3145728 | tf_op jit(solution)/shard_map/all_to_all | solution.py:272
  25.0 0.0 copy-start.1
  25.0 2.2 %collective-permute-start = (bf16[16,48,128]{2,1,0:T(8,128)(2,1)S(1)}, bf16[16,48,128]{2,1,0:T(8,128)(2,1)S(1)}, u32[]{:S(2)}, u32[]{:S(2)}) collective-permute-start(bf16[16,48,128]{2,1,0:T(8,128)(2,1)S(1)} %all-to-all-done.1.audio), channel_id=1, source_target_pairs={{16,32},{48,64},{80,96},{112,128},{144,160},{176,192},{208,224},{2... | collective-permute-start | bytes 589832 | tf_op jit(solution)/shard_map/ppermute | solution.py:249
  27.2 4.5 %collective-permute-start.1 = (bf16[16,48,128]{2,1,0:T(8,128)(2,1)S(1)}, bf16[16,48,128]{2,1,0:T(8,128)(2,1)S(1)}, u32[]{:S(2)}, u32[]{:S(2)}) collective-permute-start(bf16[16,48,128]{2,1,0:T(8,128)(2,1)S(1)} %all-to-all-done.1.audio), channel_id=1, source_target_pairs={{0,16},{32,48},{64,80},{96,112},{128,144},{160,176},{192,208},{224... | collective-permute-start | bytes 589832 | tf_op jit(solution)/shard_map/ppermute | solution.py:249
  31.7 2.8 %collective-permute-done.far = bf16[16,48,128]{2,1,0:T(8,128)(2,1)S(1)} collective-permute-done((bf16[16,48,128]{2,1,0:T(8,128)(2,1)S(1)}, bf16[16,48,128]{2,1,0:T(8,128)(2,1)S(1)}, u32[]{:S(2)}, u32[]{:S(2)}) %collective-permute-start) | collective-permute-done | bytes 196640 | tf_op jit(solution)/shard_map/ppermute | solution.py:249
  34.5 0.0 collective-permute-done.1.near
  34.5 28.5 %all-to-all-done.own = bf16[16,384,128]{2,1,0:T(8,128)(2,1)S(1)} async-done(((bf16[16,384,128]{2,1,0:T(8,128)(2,1)}), bf16[16,384,128]{2,1,0:T(8,128)(2,1)S(1)}, u32[]{:S(2)}, u32[]{:S(2)}) %all-to-all-start) | async-done | bytes 1572896 | tf_op jit(solution)/shard_map/all_to_all | solution.py:272
  63.0 3.2 %lend.1 = bf16[16,4,16,128]{3,2,1,0:T(8,128)(2,1)} custom-call(bf16[16,384,128]{2,1,0:T(8,128)(2,1)S(1)} %all-to-all-done.own, bf16[16,48,128]{2,1,0:T(8,128)(2,1)S(1)} %all-to-all-done.1.audio, bf16[16,48,128]{2,1,0:T(8,128)(2,1)S(1)} %collective-permute-done.far, bf16[16,48,128]{2,1,0:T(8,128)(2,1)S(1)} %collective-permute-done.1.near), custom_call_target="tpu_custom_call" | custom-call | flops 805306368 | bytes 2097152 | tf_op jit(solution)/shard_map/lend/pallas_call | solution.py:279
  66.2 3.5 %all-to-all-start.3 = ((bf16[16,4,16,128]{3,2,1,0:T(8,128)(2,1)}), bf16[16,4,16,128]{3,2,1,0:T(8,128)(2,1)S(1)}, u32[]{:S(2)}, u32[]{:S(2)}) async-start(bf16[16,4,16,128]{3,2,1,0:T(8,128)(2,1)} %lend.1), calls=%async_computation.3 | async-start | bytes 524288 | tf_op jit(solution)/shard_map/all_to_all | solution.py:272
  69.8 0.0 copy-done.1
  69.8 0.1 copy.6.pairs
  69.9 8.9 %attend.1 = bf16[16,128,128]{2,1,0:T(8,128)(2,1)} custom-call(s32[32,3]{1,0:T(8,128)S(1)} %copy.6.pairs, bf16[16,384,128]{2,1,0:T(8,128)(2,1)S(1)} %all-to-all-done.own, bf16[16,48,128]{2,1,0:T(8,128)(2,1)S(1)} %all-to-all-done.1.audio, bf16[16,48,128]{2,1,0:T(8,128)(2,1)S(1)} %collective-permute-done.far, bf16[16,48,128]{2,1,0:T(8,128)(2,1)S(1)} %collective-permute-done.1.near), custom_call_target="tpu_custom_call" | custom-call | flops 2952790016 | bytes 3145728 | tf_op jit(solution)/shard_map/attend/pallas_call | solution.py:295
  78.7 2.8 %all-to-all-done.3.parts = bf16[16,4,16,128]{3,2,1,0:T(8,128)(2,1)S(1)} async-done(((bf16[16,4,16,128]{3,2,1,0:T(8,128)(2,1)}), bf16[16,4,16,128]{3,2,1,0:T(8,128)(2,1)S(1)}, u32[]{:S(2)}, u32[]{:S(2)}) %all-to-all-start.3) | async-done | bytes 262176 | tf_op jit(solution)/shard_map/all_to_all | solution.py:272
  81.6 5.3 %all-to-all-start.2 = ((bf16[16,128,128]{2,1,0:T(8,128)(2,1)}), bf16[16,128,128]{2,1,0:T(8,128)(2,1)S(1)}, u32[]{:S(2)}, u32[]{:S(2)}) async-start(bf16[16,128,128]{2,1,0:T(8,128)(2,1)} %attend.1), calls=%async_computation.2 | async-start | bytes 1048576 | tf_op jit(solution)/shard_map/all_to_all | solution.py:272
  86.9 2.9 %collective-permute-start.2 = (bf16[16,2,16,128]{3,2,1,0:T(8,128)(2,1)S(1)}, bf16[16,2,16,128]{3,2,1,0:T(8,128)(2,1)S(1)}, u32[]{:S(2)}, u32[]{:S(2)}) collective-permute-start(bf16[16,2,16,128]{3,2,1,0:T(8,128)(2,1)S(1)} %get-tuple-element.3), channel_id=1, source_target_pairs={{16,32},{48,64},{80,96},{112,128},{144,160},{176,192},{208,224},{2... | collective-permute-start | bytes 393224 | tf_op jit(solution)/shard_map/ppermute | solution.py:249
  89.8 3.7 %collective-permute-start.3 = (bf16[16,2,16,128]{3,2,1,0:T(8,128)(2,1)S(1)}, bf16[16,2,16,128]{3,2,1,0:T(8,128)(2,1)S(1)}, u32[]{:S(2)}, u32[]{:S(2)}) collective-permute-start(bf16[16,2,16,128]{3,2,1,0:T(8,128)(2,1)S(1)} %get-tuple-element.2), channel_id=1, source_target_pairs={{0,16},{32,48},{64,80},{96,112},{128,144},{160,176},{192,208},{224... | collective-permute-start | bytes 393224 | tf_op jit(solution)/shard_map/ppermute | solution.py:249
  93.5 2.5 %collective-permute-done.2.from_far = bf16[16,2,16,128]{3,2,1,0:T(8,128)(2,1)S(1)} collective-permute-done((bf16[16,2,16,128]{3,2,1,0:T(8,128)(2,1)S(1)}, bf16[16,2,16,128]{3,2,1,0:T(8,128)(2,1)S(1)}, u32[]{:S(2)}, u32[]{:S(2)}) %collective-permute-start.2) | collective-permute-done | bytes 131104 | tf_op jit(solution)/shard_map/ppermute | solution.py:249
  96.0 0.0 collective-permute-done.3.from_near
  96.0 1.7 %merge.1 = bf16[16,2048]{1,0:T(8,128)(2,1)} custom-call(s32[32,3]{1,0:T(8,128)S(1)} %copy.6.pairs, bf16[16,4,16,128]{3,2,1,0:T(8,128)(2,1)S(1)} %all-to-all-done.3.parts, bf16[16,2,16,128]{3,2,1,0:T(8,128)(2,1)S(1)} %collective-permute-done.2.from_far, bf16[16,2,16,128]{3,2,1,0:T(8,128)(2,1)S(1)} %collective-permute-done.3.from_near), custom_call_target="tpu_custom_call" | custom-call | tf_op jit(solution)/shard_map/merge/pallas_call | solution.py:309
  97.7 5.8 %all-to-all-done.2.heads = bf16[16,128,128]{2,1,0:T(8,128)(2,1)S(1)} async-done(((bf16[16,128,128]{2,1,0:T(8,128)(2,1)}), bf16[16,128,128]{2,1,0:T(8,128)(2,1)S(1)}, u32[]{:S(2)}, u32[]{:S(2)}) %all-to-all-start.2) | async-done | bytes 524320 | tf_op jit(solution)/shard_map/all_to_all | solution.py:272
  103.5 0.8 unpack.1
  (1 shorter events, 0.0 us)
Async XLA Ops:
  0.6 0.9 copy-start
  2.3 19.0 %all-to-all-start.1 = ((bf16[16,48,128]{2,1,0:T(8,128)(2,1)}), bf16[16,48,128]{2,1,0:T(8,128)(2,1)S(1)}, u32[]{:S(2)}, u32[]{:S(2)}) async-start(bf16[16,48,128]{2,1,0:T(8,128)(2,1)} %bitcast.2), calls=%async_computation.1 | async-start | bytes 393216 | tf_op jit(solution)/shard_map/all_to_all | solution.py:272
  21.3 41.8 %all-to-all-start = ((bf16[16,384,128]{2,1,0:T(8,128)(2,1)}), bf16[16,384,128]{2,1,0:T(8,128)(2,1)S(1)}, u32[]{:S(2)}, u32[]{:S(2)}) async-start(bf16[16,384,128]{2,1,0:T(8,128)(2,1)} %pack_video.1), calls=%async_computation | async-start | bytes 3145728 | tf_op jit(solution)/shard_map/all_to_all | solution.py:272
  25.0 44.8 %copy-start.1 = (s32[32,3]{0,1:T(4,128)S(1)}, s32[32,3]{0,1:T(4,128)}, u32[]{:S(2)}) copy-start(s32[32,3]{0,1:T(4,128)} %param.5) | copy-start | bytes 1156
  25.0 9.5 %collective-permute-start = (bf16[16,48,128]{2,1,0:T(8,128)(2,1)S(1)}, bf16[16,48,128]{2,1,0:T(8,128)(2,1)S(1)}, u32[]{:S(2)}, u32[]{:S(2)}) collective-permute-start(bf16[16,48,128]{2,1,0:T(8,128)(2,1)S(1)} %all-to-all-done.1.audio), channel_id=1, source_target_pairs={{16,32},{48,64},{80,96},{112,128},{144,160},{176,192},{208,224},{2... | collective-permute-start | bytes 589832 | tf_op jit(solution)/shard_map/ppermute | solution.py:249
  27.2 7.3 %collective-permute-start.1 = (bf16[16,48,128]{2,1,0:T(8,128)(2,1)S(1)}, bf16[16,48,128]{2,1,0:T(8,128)(2,1)S(1)}, u32[]{:S(2)}, u32[]{:S(2)}) collective-permute-start(bf16[16,48,128]{2,1,0:T(8,128)(2,1)S(1)} %all-to-all-done.1.audio), channel_id=1, source_target_pairs={{0,16},{32,48},{64,80},{96,112},{128,144},{160,176},{192,208},{224... | collective-permute-start | bytes 589832 | tf_op jit(solution)/shard_map/ppermute | solution.py:249
  66.2 15.3 %all-to-all-start.3 = ((bf16[16,4,16,128]{3,2,1,0:T(8,128)(2,1)}), bf16[16,4,16,128]{3,2,1,0:T(8,128)(2,1)S(1)}, u32[]{:S(2)}, u32[]{:S(2)}) async-start(bf16[16,4,16,128]{3,2,1,0:T(8,128)(2,1)} %lend.1), calls=%async_computation.3 | async-start | bytes 524288 | tf_op jit(solution)/shard_map/all_to_all | solution.py:272
  81.6 22.0 %all-to-all-start.2 = ((bf16[16,128,128]{2,1,0:T(8,128)(2,1)}), bf16[16,128,128]{2,1,0:T(8,128)(2,1)S(1)}, u32[]{:S(2)}, u32[]{:S(2)}) async-start(bf16[16,128,128]{2,1,0:T(8,128)(2,1)} %attend.1), calls=%async_computation.2 | async-start | bytes 1048576 | tf_op jit(solution)/shard_map/all_to_all | solution.py:272
  86.9 9.2 %collective-permute-start.2 = (bf16[16,2,16,128]{3,2,1,0:T(8,128)(2,1)S(1)}, bf16[16,2,16,128]{3,2,1,0:T(8,128)(2,1)S(1)}, u32[]{:S(2)}, u32[]{:S(2)}) collective-permute-start(bf16[16,2,16,128]{3,2,1,0:T(8,128)(2,1)S(1)} %get-tuple-element.3), channel_id=1, source_target_pairs={{16,32},{48,64},{80,96},{112,128},{144,160},{176,192},{208,224},{2... | collective-permute-start | bytes 393224 | tf_op jit(solution)/shard_map/ppermute | solution.py:249
  89.8 6.2 %collective-permute-start.3 = (bf16[16,2,16,128]{3,2,1,0:T(8,128)(2,1)S(1)}, bf16[16,2,16,128]{3,2,1,0:T(8,128)(2,1)S(1)}, u32[]{:S(2)}, u32[]{:S(2)}) collective-permute-start(bf16[16,2,16,128]{3,2,1,0:T(8,128)(2,1)S(1)} %get-tuple-element.2), channel_id=1, source_target_pairs={{0,16},{32,48},{64,80},{96,112},{128,144},{160,176},{192,208},{224... | collective-permute-start | bytes 393224 | tf_op jit(solution)/shard_map/ppermute | solution.py:249
